TPU v7x, 512 devices: a whole 4x4x16 slice. The times are simulated.
512 devices in a mesh: fsdp: 8 (over x_lo, y), dp: 64 (over x_hi, z, core).
Axes of the slice: x: 4 (x_hi: 2, x_lo: 2; x = x_hi * 2 + x_lo), y: 4, z: 16, core: 2. Of those that a mesh axis runs over, the one named last changes fastest.
Arguments:
- values: bfloat16 [64, 1536, 2048], P('dp', 'fsdp'), may hold values from -6 to 6
- cotangent: bfloat16 [64, 1536, 2048], P('dp', 'fsdp'), may hold values from -6 to 6
- out_weight: bfloat16 [2048, 2048], P(('fsdp', 'dp')), may hold values from -0.125 to 0.125
- gate_weight: bfloat16 [256, 2048], P(None, 'fsdp'), may hold values from -0.375 to 0.375
- in_probe: bfloat16 [2048, 64], replicated, may hold values from -0.125 to 0.125
- out_probe: bfloat16 [2048, 64], replicated, may hold values from -0.125 to 0.125
- timesteps: int32 [64], P('dp'), may hold values from 0 to 999
- text_lengths: int32 [64], P('dp'), may hold values from 1 to 256
Outputs:
- mixed_out: bfloat16 [64, 1536, 2048], P('dp', 'fsdp')
- grad_values: bfloat16 [64, 1536, 2048], P('dp', 'fsdp')
- projected: float32 [64, 64, 64], P('dp', 'fsdp')
- gate_weight_grad: float32 [256, 2048], P(None, 'fsdp')
All inputs are finite; a program needn't handle non-finite values.
Results may differ from a plain program's by a relative error of at most 0.0057.
Values may be sent and summed in bfloat16 or wider, within the bound.
A program may use at most 64 MiB of HBM per device.

v0:
```python
import jax
import jax.numpy as jnp
from jax import lax
from jax.sharding import PartitionSpec as P

TXT = 256


def frequency_embedding(step_values, freq_width):
    half_width = freq_width // 2
    counter = jnp.arange(half_width, dtype=jnp.float32)
    frequencies = jnp.exp(-jnp.log(10000.0) * counter / half_width)
    angles = step_values.astype(jnp.float32)[:, None] * frequencies[None, :]
    return jnp.concatenate([jnp.cos(angles), jnp.sin(angles)], axis=-1)


def per_device(
    values, cotangent, out_weight, gate_weight, in_probe, out_probe, timesteps, text_lengths
):
    inputs_rows = values[0]
    grads_rows = cotangent[0]
    row_count = inputs_rows.shape[0]
    fsdp_count = lax.axis_size("fsdp")
    example_count = lax.axis_size("dp")
    seq_length = row_count * fsdp_count
    embedding = frequency_embedding(timesteps, gate_weight.shape[0])
    weight_full = lax.all_gather(out_weight, ("fsdp", "dp"), axis=0, tiled=True)
    gate_whole = lax.all_gather(gate_weight, "fsdp", axis=1, tiled=True)
    gate_scale = jnp.dot(embedding, gate_whole.astype(jnp.float32), precision=lax.Precision.HIGHEST)
    positions = lax.axis_index("fsdp") * row_count + jnp.arange(row_count, dtype=jnp.int32)
    row_limit = seq_length - TXT + text_lengths[0]
    valid_rows = (positions < row_limit).astype(jnp.float32)
    branch = jnp.dot(inputs_rows, weight_full, preferred_element_type=jnp.float32)
    mixed_rows = (gate_scale * branch).astype(jnp.bfloat16)
    scaled = valid_rows[:, None] * grads_rows.astype(jnp.float32)
    masked = (scaled * gate_scale).astype(jnp.bfloat16)
    grad_rows = lax.dot_general(
        masked, weight_full, (((1,), (1,)), ((), ())), preferred_element_type=jnp.float32
    ).astype(jnp.bfloat16)
    gate_local = jnp.sum(scaled * branch, axis=0)
    probe_in = jnp.dot(inputs_rows, in_probe, preferred_element_type=jnp.float32).astype(
        jnp.bfloat16
    )
    probe_out = jnp.dot(masked, out_probe, preferred_element_type=jnp.float32).astype(jnp.bfloat16)
    projected_part = lax.dot_general(
        probe_in, probe_out, (((0,), (0,)), ((), ())), preferred_element_type=jnp.float32
    ) * seq_length ** (-0.5)
    grad_scale = (seq_length * example_count) ** (-0.5)
    outer_part = embedding[0][:, None] * gate_local[None, :] * grad_scale
    projected_share, outer_share = (
        lax.psum_scatter(projected_part, "fsdp", scatter_dimension=0, tiled=True),
        lax.psum_scatter(outer_part, "fsdp", scatter_dimension=1, tiled=True),
    )
    gate_weight_grad = lax.psum(outer_share, "dp")
    return (mixed_rows[None], grad_rows[None], projected_share[None], gate_weight_grad)


def solution(mesh):
    in_specs = (
        P("dp", "fsdp", None),
        P("dp", "fsdp", None),
        P(("fsdp", "dp"), None),
        P(None, "fsdp"),
        P(),
        P(),
        P("dp"),
        P("dp"),
    )
    out_specs = (
        P("dp", "fsdp", None),
        P("dp", "fsdp", None),
        P("dp", "fsdp", None),
        P(None, "fsdp"),
    )
    return jax.shard_map(
        per_device, mesh=mesh, in_specs=in_specs, out_specs=out_specs, check_vma=False
    )
```

profile of v0, /device:TPU:6, one launch (start us, length us, event | category | flops | bytes accessed | tf_op | source)
XLA Modules:
  0.0 1440.3 jit_solution(12505087650060545376)
XLA Ops:
  7.2 0.0 all-gather.4.cloned.1.call-start
  7.2 0.7 all-gather.4.cloned.1.call-update
  7.9 0.0 all-gather.6.cloned.1.call-start
  8.0 0.7 all-gather.6.cloned.1.call-update
  8.7 0.0 reduce-scatter.2.cloned.1.call-start
  10.0 0.1 fusion.16
  10.1 49.5 %all-gather.4.cloned.1.call-done = bf16[256,2048]{1,0:T(8,128)(2,1)} async-done(((bf16[256,256]{1,0:T(8,128)(2,1)}), bf16[256,2048]{1,0:T(8,128)(2,1)}) %all-gather.4.cloned.1.call-update) | async-done | bytes 1048592 | tf_op jit(solution)/shard_map/all_gather | solution.py:28
  59.6 1.7 fusion.14
  61.3 825.6 %all-gather.6.cloned.1.call-done = bf16[512,4,2048]{2,1,0:T(4,128)(2,1)} async-done(((bf16[1,4,2048]{2,1,0:T(4,128)(2,1)}), bf16[512,4,2048]{2,1,0:T(4,128)(2,1)}) %all-gather.6.cloned.1.call-update) | async-done | bytes 8388624 | tf_op jit(solution)/shard_map/all_gather | solution.py:27
  886.9 12.5 reshape.54
  899.5 6.2 fusion.4
  905.6 1.6 multiply_multiply_fusion
  907.2 0.0 reduce-scatter.2.cloned.1.call-update
  907.2 0.0 all-reduce.3.cloned.1.call-start
  907.3 1.3 dynamic-slice
  909.3 0.4 convolution_convert_fusion.1
  909.7 0.5 fusion.6
  910.2 31.3 %all-reduce = f32[64,64]{1,0:T(8,128)S(1)} all-reduce(f32[64,64]{1,0:T(8,128)S(1)} %fusion.6), channel_id=2, replica_groups=mesh['fsdp'=8,'dp'=64] {'fsdp'}, use_global_device_ids=true, to_apply=%region_0.0.clone | all-reduce | flops 4096 | bytes 32768
  941.5 0.6 dynamic-slice_bitcast_fusion
  942.1 10.6 reduce-scatter.2.cloned.1.call-done
  952.7 0.0 all-reduce.3.cloned.1.call-update
  952.7 7.2 fusion
  959.9 472.1 %all-reduce.3.cloned.1.call-done = f32[256,256]{1,0:T(8,128)} async-done(((f32[256,256]{1,0:T(8,128)}), f32[256,256]{1,0:T(8,128)}) %all-reduce.3.cloned.1.call-update) | async-done | bytes 262160 | tf_op jit(solution)/shard_map/psum | solution.py:54
  1432.1 1.7 copy.15
  (10 shorter events, 0.0 us)
Async XLA Ops:
  7.2 892.3 %copy-start = (bf16[1,192,2048]{2,1,0:T(8,128)(2,1)S(1)}, bf16[1,192,2048]{2,1,0:T(8,128)(2,1)}, u32[]{:S(2)}) copy-start(bf16[1,192,2048]{2,1,0:T(8,128)(2,1)} %param.8) | copy-start | bytes 2359300
  7.2 52.4 %all-gather.4.cloned.1.call-start = ((), (), s32[]{:S(2)}) async-start(), calls=%async_computation.1 | async-start | bytes 1179648 | tf_op jit(solution)/shard_map/all_gather | solution.py:28
  7.9 879.0 %all-gather.6.cloned.1.call-start = ((), (), s32[]{:S(2)}) async-start(), calls=%async_computation.4 | async-start | bytes 8404992 | tf_op jit(solution)/shard_map/all_gather | solution.py:27
  8.7 944.0 %reduce-scatter.2.cloned.1.call-start = ((), (), s32[]{:S(2)}) async-start(), calls=%async_computation.2 | async-start | bytes 2359296 | tf_op jit(solution)/shard_map/reduce_scatter | solution.py:52
  61.3 838.2 %copy-start.2 = (bf16[1,192,2048]{2,1,0:T(8,128)(2,1)S(1)}, bf16[1,192,2048]{2,1,0:T(8,128)(2,1)}, u32[]{:S(2)}) copy-start(bf16[1,192,2048]{2,1,0:T(8,128)(2,1)} %param.9) | copy-start | bytes 2359300
  907.2 2.0 copy-start.3
  907.2 2.5 copy-start.1
  907.2 524.8 %all-reduce.3.cloned.1.call-start = ((), (), s32[]{:S(2)}) async-start(), calls=%async_computation.3 | async-start | bytes 524288 | tf_op jit(solution)/shard_map/psum | solution.py:54
Sparse Core Ops, SparseCore 0:
  10.0 49.4 all-gather.3
  61.8 825.1 all-gather.5
  907.4 45.3 reduce-scatter.1
  955.5 476.5 all-reduce.2
where the time goes:
time: 1440 us
  waiting for transfers between devices  1360 us (94%)
  blocking collectives  31.3 us (2%)
  local copies, waits for them, and re-layouts  16.1 us (1%)
  matrix products  16.1 us (1%)
  between operations  15.8 us (1%)
    all_gather x1, waiting for transfers between devices, per_device(): weight_full = lax.all_gather(out_weight, ('fsdp', 'dp'), axis=0, tiled=True)  826 us
    psum x1, waiting for transfers between devices, per_device(): gate_weight_grad = lax.psum(outer_share, 'dp')  472 us
    all_gather x1, waiting for transfers between devices, per_device(): gate_whole = lax.all_gather(gate_weight, 'fsdp', axis=1, tiled=True)  49.5 us
    unnamed x1, blocking collectives  31.3 us
  transfers between devices with their start and end apart: 4, of which 4 were waited for; matrix products, arithmetic and copies ran while one was open for 1% of the time, Pallas kernels for 0%

commit v1 on v0

v1 whole, which is shorter than its diff:
```python
import jax
import jax.numpy as jnp
from jax import lax
from jax.experimental import pallas as pl
from jax.experimental.pallas import tpu as pltpu
from jax.sharding import PartitionSpec as P

MESH = pl.DeviceIdType.MESH
F32, BF16 = jnp.float32, jnp.bfloat16
TXT = 256
H = 2
STEP = {0: -1, -1: 2}

AXIS = [(-1, 0), (0, -1), (1, 0), (0, 1), (2, 0), (0, 2)]
FORWARDED = [(i, -1, "A") for i in (-1, 1, 2)] + [(-1, j, "B") for j in (-1, 1, 2)]
FORWARDED = [FORWARDED[n] for n in (0, 3, 1, 4, 2, 5)]
FINAL = [(i, j, "A") for j in (1, 2) for i in (-1, 1, 2)] + [
    (i, j, "B") for i in (1, 2) for j in (-1, 1, 2)
]
FINAL = [FINAL[n] for n in (0, 6, 1, 7, 2, 8, 3, 9, 4, 10, 5, 11)]
MESSAGES = [(i, j, "AB") for i, j in AXIS] + FORWARDED + FINAL
INDEX = {message: n for n, message in enumerate(MESSAGES)}
OWN = len(MESSAGES)


def onward(message):
    i, j, part = message
    if part == "A":
        return [("yf", (i, 2, "A"))] if j == -1 else []
    if part == "B":
        return [("xf", (2, j, "B"))] if i == -1 else []
    if (i, j) == (0, 0):
        return [
            ("xf", (-1, 0, "AB")), ("yf", (0, -1, "AB")),
            ("xb", (1, 0, "AB")), ("yb", (0, 1, "AB")),
        ]
    if j == 0:
        first = [("xf", (2, 0, "AB"))] if i == -1 else []
        return first + [("yf", (i, -1, "A")), ("yb", (i, 1, "A"))]
    first = [("yf", (0, 2, "AB"))] if j == -1 else []
    return first + [("xf", (-1, j, "B")), ("xb", (1, j, "B"))]


def kernel(
    w_ref, emb_ref, len_ref, gw_ref, values_ref, cot_ref, inp_ref, outp_ref,
    mixed_out, grads_out, proj_out, gwg_out,
    wbuf, vals, cot, inp, outp, masked, mixed, grads, acc, gate,
    qbuf, psend, precv, eown, erecv, ebuf, tsend, trecv, town, t1recv, tbuf,
    l_sem, q_send, q_recv, g_send, g_recv, z_send, z_recv, x_send, x_recv, d_send, d_recv,
    p_send, p_recv, e1_send, e1_recv, e2_send, e2_recv, t0_send, t0_recv,
    t1_send, t1_recv, t2_send, t2_recv,
):
    f, d = lax.axis_index("fsdp"), lax.axis_index("dp")
    x_lo, y = f // 4, f % 4
    x_hi, z, c = d // 32, (d // 2) % 16, d % 2
    x = 2 * x_hi + x_lo
    s = 1 - 2 * c
    m, p = z // 2, z % 2

    def device(xx, yy, zz, cc):
        return ((xx % 2) * 4 + yy, (xx // 2) * 32 + zz * 2 + cc)

    def remote(src, dst, send, recv, target):
        return pltpu.make_async_remote_copy(
            src_ref=src, dst_ref=dst, send_sem=send, recv_sem=recv,
            device_id=target, device_id_type=MESH,
        )

    loads = [
        pltpu.make_async_copy(a, b, l_sem.at[n])
        for n, (a, b) in enumerate(
            ((values_ref, vals), (cot_ref, cot), (inp_ref, inp), (outp_ref, outp))
        )
    ]
    for load in loads:
        load.start()

    here = (f, d)
    core_peer = device(x, y, z, 1 - c)
    z_peers = [device(x, y, (z + k) % 16, c) for k in range(1, 16)]
    f_peers = [((f + k) % 8, d) for k in range(1, 8)]
    quad_peers = []
    for k in range(1, 4):
        t = (2 * x_hi + c + k) % 4
        quad_peers.append((f, (t // 2) * 32 + z * 2 + t % 2))
    way = {
        "xf": device((x + s + 4) % 4, y, z, c),
        "xb": device((x - s + 4) % 4, y, z, c),
        "yf": device(x, (y + s + 4) % 4, z, c),
        "yb": device(x, (y - s + 4) % 4, z, c),
    }

    barrier = pltpu.get_barrier_semaphore()
    greeted = z_peers + f_peers + quad_peers
    greeted = greeted + [
        (f, x_hi * 32 + (z + 1 - 2 * p) * 2 + 1 - c),
        ((1 - x_lo) * 4 + y, (1 - x_hi) * 32 + z * 2 + c),
    ]
    for peer in greeted:
        pl.semaphore_signal(barrier, inc=1, device_id=peer, device_id_type=MESH)

    mine = w_ref[...].astype(F32)
    t_own = 2 * p + c
    qbuf[t_own] = jnp.concatenate(
        [mine[:, 512 * n : 512 * n + 512] for n in range(4)], axis=0
    ).astype(BF16)
    pl.semaphore_wait(barrier, len(greeted))

    q_copies = []
    for k in range(1, 4):
        t = (t_own + k) % 4
        target = device(x, y, 2 * m + t // 2, t % 2)
        copy = remote(qbuf.at[t_own], qbuf.at[t_own], q_send.at[k], q_recv.at[k], target)
        copy.start()
        q_copies.append(copy)

    emb = emb_ref[...]
    share = jnp.dot(
        jnp.broadcast_to(emb, (8, 256)), gw_ref[...].astype(F32),
        precision=lax.Precision.HIGHEST, preferred_element_type=F32,
    )
    f_cols = pl.ds(pl.multiple_of(256 * f, 256), 256)
    gate[:, f_cols] = share
    g_copies = []
    for k in range(1, 8):
        copy = remote(gate.at[:, f_cols], gate.at[:, f_cols], g_send.at[k], g_recv.at[k], f_peers[k - 1])
        copy.start()
        g_copies.append(copy)

    for copy in q_copies:
        copy.wait_recv()
    quarter = [qbuf[t].astype(F32) for t in range(4)]
    low, high = [
        jnp.concatenate(
            [
                jnp.concatenate([quarter[t][4 * n : 4 * n + 4] for t in range(4)], axis=0)
                for n in pair
            ],
            axis=1,
        )
        for pair in ((0, 1), (2, 3))
    ]

    def row_of(i, j):
        xx, yy = (x + s * i + 8) % 4, (y + s * j + 8) % 4
        return (xx % 2) * 1024 + yy * 256 + (xx // 2) * 128

    def cols_of(core, h, part):
        start = 1024 * core + (1024 // H) * h + (512 // H if part == "B" else 0)
        width = 1024 // H if part == "AB" else 512 // H
        return pl.ds(pl.multiple_of(start, 128), width)

    own_rows = pl.ds(pl.multiple_of(row_of(0, 0) + 16 * m, 16), 16)
    half_cols = pl.ds(pl.multiple_of(1024 * c, 1024), 1024)
    wbuf[own_rows, half_cols] = jnp.where(c == 0, low, high).astype(BF16)

    sent = []
    z_copies = {}
    for h in range(H):
        cols = cols_of(c, h, "AB")
        block = wbuf.at[own_rows, cols]
        for k in range(1, 8):
            to = (z + (2 * p - 1) * k + 16) % 16
            away = (to // 2 - m + 8) % 8
            copy = remote(block, block, z_send.at[h, k], z_recv.at[h, away], device(x, y, to, c))
            copy.start()
            sent.append(copy)

    def z_wait(h):
        block = wbuf.at[own_rows, cols_of(c, h, "AB")]
        for away in range(1, 8):
            remote(block, block, z_send.at[h, away], z_recv.at[h, away], core_peer).wait_recv()

    def block_of(core, h, message):
        i, j, part = message
        rows = pl.ds(pl.multiple_of(row_of(i, j), 128), 128)
        return wbuf.at[rows, cols_of(core, h, part)]


    def part_block(h, message, part):
        return block_of(c, h, (message[0], message[1], part))

    def forward(h, message):
        i, j, part = message
        for direction, there in onward(message):
            n = INDEX[there]
            block = part_block(h, message, there[2])
            copy = remote(block, block, x_send.at[h, n], x_recv.at[h, n], way[direction])
            copy.start()
            sent.append(copy)
        n = OWN if (i, j) == (0, 0) else INDEX[message]
        block = block_of(c, h, message)
        copy = remote(block, block, d_send.at[h, n], d_recv.at[h, n], core_peer)
        copy.start()
        sent.append(copy)

    def take(h, message):
        n = INDEX[message]
        block = block_of(c, h, message)
        remote(block, block, x_send.at[h, n], x_recv.at[h, n], core_peer).wait_recv()
        forward(h, message)

    def other_core(h):
        for n, message in enumerate(MESSAGES + [(0, 0, "AB")]):
            block = block_of(1 - c, h, message)
            remote(block, block, d_send.at[h, n], d_recv.at[h, n], core_peer).wait_recv()

    e = 2 * x_hi + c
    tile_row = lax.broadcasted_iota(jnp.int32, (8, 128), 0)

    def tile_of(row):
        low = jnp.broadcast_to(row[:, :128], (8, 128))
        high = jnp.broadcast_to(row[:, 128:], (8, 128))
        zero = jnp.zeros((8, 128), F32)
        return jnp.where(tile_row == e, low, jnp.where(tile_row == e + 4, high, zero))

    eown[...] = tile_of(emb)
    e_copies = []
    for k in range(1, 4):
        copy = remote(eown, erecv.at[k], e1_send.at[k], e1_recv.at[k], quad_peers[k - 1])
        copy.start()
        e_copies.append(copy)

    z_wait(0)
    forward(0, (0, 0, "AB"))

    for copy in g_copies:
        copy.wait_recv()
    for load in loads:
        load.wait()
    limit = 8 * 192 - TXT + len_ref[0]

    def valid(width):
        return lax.broadcasted_iota(jnp.int32, (192, width), 0) + f * 192 < limit

    @pl.loop(0, 8)
    def _(n):
        cols = pl.ds(pl.multiple_of(n * 256, 256), 256)
        scaled = jnp.where(valid(256), cot[:, cols].astype(F32), 0.0)
        masked[:, cols] = (scaled * gate[0:1, cols]).astype(BF16)

    for i, j in AXIS:
        take(0, (i, j, "AB"))
    z_wait(1)
    forward(1, (0, 0, "AB"))
    for message in FORWARDED:
        take(0, message)

    for copy in e_copies:
        copy.wait_recv()
    ebuf[z] = eown[...] + erecv[1] + erecv[2] + erecv[3]
    e2_copies = []
    for k in range(1, 16):
        copy = remote(ebuf.at[z], ebuf.at[z], e2_send.at[k], e2_recv.at[k], z_peers[k - 1])
        copy.start()
        e2_copies.append(copy)

    for i, j in AXIS:
        take(1, (i, j, "AB"))

    probe_in = jnp.dot(vals[...], inp[...], preferred_element_type=F32).astype(BF16)
    probe_out = jnp.dot(masked[...], outp[...], preferred_element_type=F32).astype(BF16)
    projected = lax.dot_general(
        probe_in, probe_out, (((0,), (0,)), ((), ())), preferred_element_type=F32
    ) * (8 * 192) ** (-0.5)
    psend[...] = projected.reshape(8, 8, 64)
    p_copies = []
    for k in range(1, 8):
        copy = remote(psend.at[(f + k) % 8], precv.at[k], p_send.at[k], p_recv.at[k], f_peers[k - 1])
        copy.start()
        p_copies.append(copy)

    for message in FINAL:
        take(0, message)
    for message in FORWARDED:
        take(1, message)

    def branch(start):
        cols = pl.ds(pl.multiple_of(start, 256), 256)
        product = jnp.dot(vals[...], wbuf[:, cols], preferred_element_type=F32)
        mixed[:, cols] = (product * gate[0:1, cols]).astype(BF16)
        scaled = jnp.where(valid(256), cot[:, cols].astype(F32), 0.0)
        tsend[start // 256] = tile_of(jnp.sum(scaled * product, axis=0, keepdims=True))

    def branches(h):
        @pl.loop(0, 4)
        def _(n):
            branch((n // 2) * 1024 + h * 512 + (n % 2) * 256)

    def grad(h, n):
        rows = pl.ds(pl.multiple_of(n * 256, 256), 256)
        total = 0.0 if h == 0 else acc[:, rows]
        for core in range(2):
            cols = slice(1024 * core + 512 * h, 1024 * core + 512 * h + 512)
            total = total + lax.dot_general(
                masked[:, cols], wbuf[rows, cols], (((1,), (1,)), ((), ())),
                preferred_element_type=F32,
            )
        if h == 0:
            acc[:, rows] = total
        else:
            grads[:, rows] = total.astype(BF16)

    other_core(0)
    branches(0)
    for n in range(0, 6):
        take(1, FINAL[n])
    pl.loop(0, 8)(lambda n: grad(0, n))
    for n in range(6, 12):
        take(1, FINAL[n])

    other_core(1)
    branches(1)
    store_mixed = pltpu.make_async_copy(mixed, mixed_out, l_sem.at[4])
    store_mixed.start()

    t0_copies = []
    for k in range(1, 8):
        copy = remote(tsend.at[(f + k) % 8], trecv.at[k], t0_send.at[k], t0_recv.at[k], f_peers[k - 1])
        copy.start()
        t0_copies.append(copy)
    pl.loop(0, 4)(lambda n: grad(1, n))
    total = tsend[f]
    for k in range(1, 8):
        t0_copies[k - 1].wait_recv()
        total = total + trecv[k]
    town[...] = total
    t1_copies = []
    for k in range(1, 4):
        copy = remote(town, t1recv.at[k], t1_send.at[k], t1_recv.at[k], quad_peers[k - 1])
        copy.start()
        t1_copies.append(copy)
    pl.loop(4, 8)(lambda n: grad(1, n))
    store_grads = pltpu.make_async_copy(grads, grads_out, l_sem.at[5])
    store_grads.start()
    for copy in t1_copies:
        copy.wait_recv()
    tbuf[z] = town[...] + t1recv[1] + t1recv[2] + t1recv[3]
    t2_copies = []
    for k in range(1, 16):
        copy = remote(tbuf.at[z], tbuf.at[z], t2_send.at[k], t2_recv.at[k], z_peers[k - 1])
        copy.start()
        t2_copies.append(copy)

    total = psend[f]
    for k in range(1, 8):
        p_copies[k - 1].wait_recv()
        total = total + precv[k]
    proj_out[...] = total
    for copy in q_copies + g_copies + sent + e_copies + e2_copies + p_copies + t0_copies + t1_copies:
        copy.wait_send()
    for copy in e2_copies:
        copy.wait_recv()
    for copy in t2_copies:
        copy.wait()

    emb_all = ebuf[...].reshape(128, 128)
    grad_all = tbuf[...].reshape(128, 128)
    in_high = lax.broadcasted_iota(jnp.int32, (128, 128), 0) % 8 >= 4
    for half in range(2):
        ours = jnp.where(in_high if half else jnp.logical_not(in_high), grad_all, 0.0)
        for k_half in range(2):
            rows = emb_all
            if k_half != half:
                rows = pltpu.roll(emb_all, 4 if half else 124, 0)
            gwg_out[128 * k_half : 128 * k_half + 128, 128 * half : 128 * half + 128] = (
                lax.dot_general(
                    rows, ours, (((0,), (0,)), ((), ())),
                    precision=lax.Precision.HIGHEST, preferred_element_type=F32,
                ) * (8 * 192 * 64) ** (-0.5)
            )
    store_mixed.wait()
    store_grads.wait()


def frequency_embedding(step_values, freq_width):
    half_width = freq_width // 2
    counter = jnp.arange(half_width, dtype=jnp.float32)
    frequencies = jnp.exp(-jnp.log(10000.0) * counter / half_width)
    angles = step_values.astype(jnp.float32)[:, None] * frequencies[None, :]
    return jnp.concatenate([jnp.cos(angles), jnp.sin(angles)], axis=-1)


def per_device(
    values, cotangent, out_weight, gate_weight, in_probe, out_probe, timesteps, text_lengths
):
    embedding = frequency_embedding(timesteps, 256)
    vmem = pl.BlockSpec(memory_space=pltpu.VMEM)
    smem = pl.BlockSpec(memory_space=pltpu.SMEM)
    anywhere = pl.BlockSpec(memory_space=pl.ANY)
    dma = pltpu.SemaphoreType.DMA
    count = OWN + 1
    mixed, grads, projected, gwg = pl.pallas_call(
        kernel,
        out_shape=(
            jax.ShapeDtypeStruct((192, 2048), BF16),
            jax.ShapeDtypeStruct((192, 2048), BF16),
            jax.ShapeDtypeStruct((8, 64), F32),
            jax.ShapeDtypeStruct((256, 256), F32),
        ),
        in_specs=[vmem, vmem, smem, vmem, anywhere, anywhere, anywhere, anywhere],
        out_specs=(anywhere, anywhere, vmem, vmem),
        scratch_shapes=[
            pltpu.VMEM((2048, 2048), BF16),
            pltpu.VMEM((192, 2048), BF16),
            pltpu.VMEM((192, 2048), BF16),
            pltpu.VMEM((2048, 64), BF16),
            pltpu.VMEM((2048, 64), BF16),
            pltpu.VMEM((192, 2048), BF16),
            pltpu.VMEM((192, 2048), BF16),
            pltpu.VMEM((192, 2048), BF16),
            pltpu.VMEM((192, 2048), F32),
            pltpu.VMEM((8, 2048), F32),
            pltpu.VMEM((4, 16, 512), BF16),
            pltpu.VMEM((8, 8, 64), F32),
            pltpu.VMEM((8, 8, 64), F32),
            pltpu.VMEM((8, 128), F32),
            pltpu.VMEM((4, 8, 128), F32),
            pltpu.VMEM((16, 8, 128), F32),
            pltpu.VMEM((8, 8, 128), F32),
            pltpu.VMEM((8, 8, 128), F32),
            pltpu.VMEM((8, 128), F32),
            pltpu.VMEM((4, 8, 128), F32),
            pltpu.VMEM((16, 8, 128), F32),
            dma((6,)),
            dma((4,)), dma((4,)),
            dma((8,)), dma((8,)),
            dma((H, 8)), dma((H, 8)),
            dma((H, count)), dma((H, count)),
            dma((H, count)), dma((H, count)),
            dma((8,)), dma((8,)),
            dma((4,)), dma((4,)),
            dma((16,)), dma((16,)),
            dma((8,)), dma((8,)),
            dma((4,)), dma((4,)),
            dma((16,)), dma((16,)),
        ],
        compiler_params=pltpu.CompilerParams(
            collective_id=0, has_side_effects=True, vmem_limit_bytes=40 * 1024 * 1024
        ),
        cost_estimate=pl.CostEstimate(
            flops=4 * 192 * 2048 * 2048, bytes_accessed=8 * 192 * 2048, transcendentals=0
        ),
    )(
        out_weight, embedding, text_lengths, gate_weight,
        values[0], cotangent[0], in_probe, out_probe,
    )
    return mixed[None], grads[None], projected[None], gwg


def solution(mesh):
    in_specs = (
        P("dp", "fsdp", None),
        P("dp", "fsdp", None),
        P(("fsdp", "dp"), None),
        P(None, "fsdp"),
        P(),
        P(),
        P("dp"),
        P("dp"),
    )
    out_specs = (
        P("dp", "fsdp", None),
        P("dp", "fsdp", None),
        P("dp", "fsdp", None),
        P(None, "fsdp"),
    )
    return jax.shard_map(
        per_device, mesh=mesh, in_specs=in_specs, out_specs=out_specs, check_vma=False
    )
```

time: 1440 us -> 92.3 us (0.06)
  waiting for transfers between devices: 1360 us -> 0 us
  Pallas kernels: 0 us -> 82.8 us
  blocking collectives: 31.3 us -> 0 us
  matrix products: 16.1 us -> 0 us
    all_gather x2 -> x0, waiting for transfers between devices: 875 us -> none  [the longest x1 826 us: per_device(): weight_full = lax.all_gather(out_weight, ('fsdp', 'dp'), axis=0, tiled=True)]
    psum x1 -> x0, waiting for transfers between devices: 472 us -> none  [per_device(): gate_weight_grad = lax.psum(outer_share, 'dp')]
    pallas_call x0 -> x1, Pallas kernels: none -> 82.8 us  [per_device(): pl.pallas_call(kernel, out_shape=(jax.ShapeDtypeStruct((192, 2048), BF16)...]
    unnamed x1 -> x0, blocking collectives: 31.3 us -> none
    dot_general x5 -> x0, matrix products: 16.1 us -> none  [the longest x1 7.2 us: per_device(): lax.dot_general(masked, weight_full, (((1,), (1,)), ((), ())), preferred_...]
  transfers between devices with their start and end apart: 4 -> 0, of which waited for: 4 -> 0; matrix products, arithmetic and copies ran while one was open for 1% -> 0% of each run, Pallas kernels for 0% -> 0%
where the time goes in v1:
time: 92.3 us; the launch traced here: 91.4 us
  Pallas kernels  82.8 us (90%)
  local copies, waits for them, and re-layouts  6.54 us (7%)
  between operations  2.03 us (2%)
    pallas_call x1, Pallas kernels, per_device(): pl.pallas_call(kernel, out_shape=(jax.ShapeDtypeStruct((192, 2048), BF16)...  82.8 us
    unnamed x14, local copies, waits for them, and re-layouts  6.54 us

profile of v1, /device:TPU:6, one launch (start us, length us, event | category | flops | bytes accessed | tf_op | source)
XLA Modules:
  0.0 91.4 jit_solution(14320469213612198045)
XLA Ops:
  1.3 0.0 copy-start.3
  1.9 0.1 fusion
  2.0 0.0 copy-start
  2.0 0.0 copy-start.1
  2.0 1.3 %copy.12.inp_ref = bf16[2048,64]{1,0:T(8,128)(2,1)S(1)} copy(bf16[2048,64]{0,1:T(8,128)(2,1)} %param.12) | data formatting | bytes 524288 | tf_op args[4]
  3.4 1.2 %copy.13.outp_ref = bf16[2048,64]{1,0:T(8,128)(2,1)S(1)} copy(bf16[2048,64]{0,1:T(8,128)(2,1)} %param.13) | data formatting | bytes 524288 | tf_op args[5]
  4.6 0.0 copy-done.3
  4.6 0.0 copy-done
  4.6 0.0 copy-done.1
  4.6 0.0 copy-start.2
  4.7 0.9 copy-done.2
  5.6 82.8 %shard_map.111 = (bf16[192,2048]{1,0:T(8,128)(2,1)S(1)}, bf16[192,2048]{1,0:T(8,128)(2,1)S(1)}, f32[8,64]{1,0:T(8,128)S(1)}, f32[256,256]{1,0:T(8,128)S(1)}) custom-call(bf16[4,2048]{1,0:T(4,128)(2,1)S(1)} %copy-done.3, f32[1,256]{1,0:T(1,128)S(1)} %pad_maximum_fusion.emb_ref, s32[1]{0:T(128)S(6)} %copy.19.len_ref, bf16[256,256]{1,0:T(8,128)(2,1)S(1)} %copy-done.2, ...), custom_call_target="tpu_custom_call" | custom-call | flops 3221225472 | bytes 3145728 | tf_op jit(solution)/shard_map/pallas_call | solution.py:393
  88.3 0.9 copy.20
  89.2 0.9 copy.21
  90.1 0.6 copy.22
  90.7 0.7 copy.23
  (1 shorter events, 0.0 us)
Async XLA Ops:
  1.3 3.3 %copy-start.3 = (bf16[4,2048]{1,0:T(4,128)(2,1)S(1)}, bf16[4,2048]{1,0:T(4,128)(2,1)}, u32[]{:S(2)}) copy-start(bf16[4,2048]{1,0:T(4,128)(2,1)} %w_ref.1) | copy-start | bytes 49156
  2.0 2.6 %copy-start = (bf16[1,192,2048]{2,1,0:T(8,128)(2,1)S(1)}, bf16[1,192,2048]{2,1,0:T(8,128)(2,1)}, u32[]{:S(2)}) copy-start(bf16[1,192,2048]{2,1,0:T(8,128)(2,1)} %param.8) | copy-start | bytes 2359300
  2.0 2.6 %copy-start.1 = (bf16[1,192,2048]{2,1,0:T(8,128)(2,1)S(1)}, bf16[1,192,2048]{2,1,0:T(8,128)(2,1)}, u32[]{:S(2)}) copy-start(bf16[1,192,2048]{2,1,0:T(8,128)(2,1)} %param.9) | copy-start | bytes 2359300
  4.6 0.9 copy-start.2

commit v2 on v1

--- a/solution.py
+++ b/solution.py
@@ -8,8 +8,9 @@
 MESH = pl.DeviceIdType.MESH
 F32, BF16 = jnp.float32, jnp.bfloat16
 TXT = 256
-H = 2
-STEP = {0: -1, -1: 2}
+GROUPS = ((0, 48), (48, 80))
+SLOTS = ((1, 2), (3, 4, 5, 6, 7))
+H = len(GROUPS)
 
 AXIS = [(-1, 0), (0, -1), (1, 0), (0, 1), (2, 0), (0, 2)]
 FORWARDED = [(i, -1, "A") for i in (-1, 1, 2)] + [(-1, j, "B") for j in (-1, 1, 2)]
@@ -18,6 +19,9 @@
     (i, j, "B") for i in (1, 2) for j in (-1, 1, 2)
 ]
 FINAL = [FINAL[n] for n in (0, 6, 1, 7, 2, 8, 3, 9, 4, 10, 5, 11)]
+SIDE = [message for message in FINAL if message[:2] in ((-1, 1), (1, 1), (1, -1), (1, 2), (2, 1))]
+SIDE = [message for message in SIDE if message not in ((1, 2, "A"), (2, 1, "B"))]
+LAST = [message for message in FINAL if message not in SIDE]
 MESSAGES = [(i, j, "AB") for i, j in AXIS] + FORWARDED + FINAL
 INDEX = {message: n for n, message in enumerate(MESSAGES)}
 OWN = len(MESSAGES)
@@ -44,11 +48,10 @@
 def kernel(
     w_ref, emb_ref, len_ref, gw_ref, values_ref, cot_ref, inp_ref, outp_ref,
     mixed_out, grads_out, proj_out, gwg_out,
-    wbuf, vals, cot, inp, outp, masked, mixed, grads, acc, gate,
-    qbuf, psend, precv, eown, erecv, ebuf, tsend, trecv, town, t1recv, tbuf,
+    wbuf, vals, cot, inp, outp, gw, valsp, place, masked, mixed, grads, acc, gate,
+    qbuf, psend, precv, eown, erecv, ebuf, tsend, trecv, tbuf,
     l_sem, q_send, q_recv, g_send, g_recv, z_send, z_recv, x_send, x_recv, d_send, d_recv,
-    p_send, p_recv, e1_send, e1_recv, e2_send, e2_recv, t0_send, t0_recv,
-    t1_send, t1_recv, t2_send, t2_recv,
+    p_send, p_recv, e1_send, e1_recv, e2_send, e2_recv, t1_send, t1_recv, t2_send, t2_recv,
 ):
     f, d = lax.axis_index("fsdp"), lax.axis_index("dp")
     x_lo, y = f // 4, f % 4
@@ -69,7 +72,7 @@
     loads = [
         pltpu.make_async_copy(a, b, l_sem.at[n])
         for n, (a, b) in enumerate(
-            ((values_ref, vals), (cot_ref, cot), (inp_ref, inp), (outp_ref, outp))
+            ((gw_ref, gw), (values_ref, vals), (cot_ref, cot), (inp_ref, inp), (outp_ref, outp))
         )
     ]
     for load in loads:
@@ -115,8 +118,9 @@
         q_copies.append(copy)
 
     emb = emb_ref[...]
+    loads[0].wait()
     share = jnp.dot(
-        jnp.broadcast_to(emb, (8, 256)), gw_ref[...].astype(F32),
+        jnp.broadcast_to(emb, (8, 256)), gw[...].astype(F32),
         precision=lax.Precision.HIGHEST, preferred_element_type=F32,
     )
     f_cols = pl.ds(pl.multiple_of(256 * f, 256), 256)
@@ -145,36 +149,37 @@
         xx, yy = (x + s * i + 8) % 4, (y + s * j + 8) % 4
         return (xx % 2) * 1024 + yy * 256 + (xx // 2) * 128
 
-    def cols_of(core, h, part):
-        start = 1024 * core + (1024 // H) * h + (512 // H if part == "B" else 0)
-        width = 1024 // H if part == "AB" else 512 // H
-        return pl.ds(pl.multiple_of(start, 128), width)
-
-    own_rows = pl.ds(pl.multiple_of(row_of(0, 0) + 16 * m, 16), 16)
-    half_cols = pl.ds(pl.multiple_of(1024 * c, 1024), 1024)
+    def cols_of(core, part):
+        start = 1024 * core + (512 if part == "B" else 0)
+        return pl.ds(pl.multiple_of(start, 512), 1024 if part == "AB" else 512)
+
+    own = row_of(0, 0)
+    own_rows = pl.ds(pl.multiple_of(own, 16), 16)
+    half_cols = cols_of(c, "AB")
     wbuf[own_rows, half_cols] = jnp.where(c == 0, low, high).astype(BF16)
 
     sent = []
-    z_copies = {}
-    for h in range(H):
-        cols = cols_of(c, h, "AB")
-        block = wbuf.at[own_rows, cols]
-        for k in range(1, 8):
-            to = (z + (2 * p - 1) * k + 16) % 16
-            away = (to // 2 - m + 8) % 8
-            copy = remote(block, block, z_send.at[h, k], z_recv.at[h, away], device(x, y, to, c))
-            copy.start()
-            sent.append(copy)
+    for k in range(1, 8):
+        away = (k + 1) // 2
+        slot = 2 * away - 1 + (p if away < 4 else 0)
+        there = pl.ds(pl.multiple_of(own + 16 * slot, 16), 16)
+        copy = remote(
+            wbuf.at[own_rows, half_cols], wbuf.at[there, half_cols], z_send.at[k], z_recv.at[slot],
+            device(x, y, (z + (2 * p - 1) * k + 16) % 16, c),
+        )
+        copy.start()
+        sent.append(copy)
 
     def z_wait(h):
-        block = wbuf.at[own_rows, cols_of(c, h, "AB")]
-        for away in range(1, 8):
-            remote(block, block, z_send.at[h, away], z_recv.at[h, away], core_peer).wait_recv()
+        for slot in SLOTS[h]:
+            block = wbuf.at[pl.ds(pl.multiple_of(own + 16 * slot, 16), 16), half_cols]
+            remote(block, block, z_send.at[slot], z_recv.at[slot], core_peer).wait_recv()
 
     def block_of(core, h, message):
         i, j, part = message
-        rows = pl.ds(pl.multiple_of(row_of(i, j), 128), 128)
-        return wbuf.at[rows, cols_of(core, h, part)]
+        first, count = GROUPS[h]
+        rows = pl.ds(pl.multiple_of(row_of(i, j) + first, 16), count)
+        return wbuf.at[rows, cols_of(core, part)]
 
 
     def part_block(h, message, part):
@@ -200,10 +205,13 @@
         remote(block, block, x_send.at[h, n], x_recv.at[h, n], core_peer).wait_recv()
         forward(h, message)
 
-    def other_core(h):
-        for n, message in enumerate(MESSAGES + [(0, 0, "AB")]):
-            block = block_of(1 - c, h, message)
-            remote(block, block, d_send.at[h, n], d_recv.at[h, n], core_peer).wait_recv()
+    def from_other_core(i, j):
+        i_there, j_there = (-i if i % 2 else i), (-j if j % 2 else j)
+        for h in range(H):
+            for part in ("AB",) if 0 in (i, j) else ("A", "B"):
+                n = OWN if (i, j) == (0, 0) else INDEX[(i_there, j_there, part)]
+                block = block_of(1 - c, h, (i, j, part))
+                remote(block, block, d_send.at[h, n], d_recv.at[h, n], core_peer).wait_recv()
 
     e = 2 * x_hi + c
     tile_row = lax.broadcasted_iota(jnp.int32, (8, 128), 0)
@@ -226,7 +234,7 @@
 
     for copy in g_copies:
         copy.wait_recv()
-    for load in loads:
+    for load in loads[1:]:
         load.wait()
     limit = 8 * 192 - TXT + len_ref[0]
 
@@ -238,6 +246,19 @@
         cols = pl.ds(pl.multiple_of(n * 256, 256), 256)
         scaled = jnp.where(valid(256), cot[:, cols].astype(F32), 0.0)
         masked[:, cols] = (scaled * gate[0:1, cols]).astype(BF16)
+
+    k_at = lax.broadcasted_iota(jnp.int32, (128, 128), 0)
+    n_at = lax.broadcasted_iota(jnp.int32, (128, 128), 1)
+    slot_at = n_at // 16
+    away_at = jnp.where(slot_at % 2 == 1, (slot_at + 1) // 2, 8 - slot_at // 2)
+    place[...] = jnp.where(k_at == (m + away_at) % 8 * 16 + n_at % 16, 1.0, 0.0).astype(BF16)
+
+    @pl.loop(0, 16)
+    def _(n):
+        cols = pl.ds(pl.multiple_of(n * 128, 128), 128)
+        valsp[:, cols] = jnp.dot(
+            vals[:, cols], place[...], preferred_element_type=F32
+        ).astype(BF16)
 
     for i, j in AXIS:
         take(0, (i, j, "AB"))
@@ -258,8 +279,9 @@
     for i, j in AXIS:
         take(1, (i, j, "AB"))
 
-    probe_in = jnp.dot(vals[...], inp[...], preferred_element_type=F32).astype(BF16)
-    probe_out = jnp.dot(masked[...], outp[...], preferred_element_type=F32).astype(BF16)
+    turned = (((1,), (1,)), ((), ()))
+    probe_in = lax.dot_general(vals[...], inp[...], turned, preferred_element_type=F32).astype(BF16)
+    probe_out = lax.dot_general(masked[...], outp[...], turned, preferred_element_type=F32).astype(BF16)
     projected = lax.dot_general(
         probe_in, probe_out, (((0,), (0,)), ((), ())), preferred_element_type=F32
     ) * (8 * 192) ** (-0.5)
@@ -272,70 +294,85 @@
 
     for message in FINAL:
         take(0, message)
+
+    def pair_rows(i, j):
+        xx, yy = (x + i + 8) % 2, (y + s * j + 8) % 4
+        return pl.ds(pl.multiple_of(xx * 1024 + yy * 256, 256), 256)
+
+    def branch(i, j, first=False):
+        rows = pair_rows(i, j)
+
+        @pl.loop(0, 8)
+        def _(n):
+            cols = pl.ds(pl.multiple_of(n * 256, 256), 256)
+            product = jnp.dot(valsp[:, rows], wbuf[rows, cols], preferred_element_type=F32)
+            acc[:, cols] = product if first else acc[:, cols] + product
+
+    def grad(i, j):
+        rows = pair_rows(i, j)
+        slots = lax.dot_general(
+            masked[...], wbuf[rows, :], turned, preferred_element_type=F32
+        ).astype(BF16)
+        for n in range(2):
+            cols = pl.ds(pl.multiple_of(rows.start + 128 * n, 128), 128)
+            grads[:, cols] = lax.dot_general(
+                slots[:, 128 * n : 128 * n + 128], place[...], turned, preferred_element_type=F32
+            ).astype(BF16)
+
+    def pair_wait(i, j):
+        for i_each in (0, 2) if i == 0 else (-1, 1):
+            from_other_core(i_each, j)
+
     for message in FORWARDED:
         take(1, message)
-
-    def branch(start):
-        cols = pl.ds(pl.multiple_of(start, 256), 256)
-        product = jnp.dot(vals[...], wbuf[:, cols], preferred_element_type=F32)
+    pair_wait(0, 0)
+    branch(0, 0, first=True)
+    pair_wait(1, 0)
+    branch(1, 0)
+    for message in SIDE:
+        take(1, message)
+    grad(0, 0)
+    grad(1, 0)
+    for j in (-1, 1):
+        pair_wait(1, j)
+        branch(1, j)
+        grad(1, j)
+    for message in LAST:
+        take(1, message)
+    for i, j in ((0, -1), (0, 1), (1, 2), (0, 2)):
+        pair_wait(i, j)
+        branch(i, j)
+
+    @pl.loop(0, 8)
+    def _(n):
+        cols = pl.ds(pl.multiple_of(n * 256, 256), 256)
+        product = acc[:, cols]
+        scaled = jnp.where(valid(256), cot[:, cols].astype(F32), 0.0)
+        tsend[n] = tile_of(jnp.sum(scaled * product, axis=0, keepdims=True))
         mixed[:, cols] = (product * gate[0:1, cols]).astype(BF16)
-        scaled = jnp.where(valid(256), cot[:, cols].astype(F32), 0.0)
-        tsend[start // 256] = tile_of(jnp.sum(scaled * product, axis=0, keepdims=True))
-
-    def branches(h):
-        @pl.loop(0, 4)
-        def _(n):
-            branch((n // 2) * 1024 + h * 512 + (n % 2) * 256)
-
-    def grad(h, n):
-        rows = pl.ds(pl.multiple_of(n * 256, 256), 256)
-        total = 0.0 if h == 0 else acc[:, rows]
-        for core in range(2):
-            cols = slice(1024 * core + 512 * h, 1024 * core + 512 * h + 512)
-            total = total + lax.dot_general(
-                masked[:, cols], wbuf[rows, cols], (((1,), (1,)), ((), ())),
-                preferred_element_type=F32,
-            )
-        if h == 0:
-            acc[:, rows] = total
-        else:
-            grads[:, rows] = total.astype(BF16)
-
-    other_core(0)
-    branches(0)
-    for n in range(0, 6):
-        take(1, FINAL[n])
-    pl.loop(0, 8)(lambda n: grad(0, n))
-    for n in range(6, 12):
-        take(1, FINAL[n])
-
-    other_core(1)
-    branches(1)
-    store_mixed = pltpu.make_async_copy(mixed, mixed_out, l_sem.at[4])
+
+    t1_copies = []
+    for k in range(8):
+        to_f = (f + k) % 8
+        for k_quad in range(4):
+            n = 4 * k + k_quad
+            if n:
+                t = (e + k_quad) % 4
+                target = (to_f, (t // 2) * 32 + z * 2 + t % 2)
+                copy = remote(tsend.at[to_f], trecv.at[n], t1_send.at[n], t1_recv.at[n], target)
+                copy.start()
+                t1_copies.append(copy)
+    store_mixed = pltpu.make_async_copy(mixed, mixed_out, l_sem.at[5])
     store_mixed.start()
-
-    t0_copies = []
-    for k in range(1, 8):
-        copy = remote(tsend.at[(f + k) % 8], trecv.at[k], t0_send.at[k], t0_recv.at[k], f_peers[k - 1])
-        copy.start()
-        t0_copies.append(copy)
-    pl.loop(0, 4)(lambda n: grad(1, n))
+    for i, j in ((0, -1), (0, 1), (1, 2), (0, 2)):
+        grad(i, j)
+    store_grads = pltpu.make_async_copy(grads, grads_out, l_sem.at[6])
+    store_grads.start()
     total = tsend[f]
-    for k in range(1, 8):
-        t0_copies[k - 1].wait_recv()
-        total = total + trecv[k]
-    town[...] = total
-    t1_copies = []
-    for k in range(1, 4):
-        copy = remote(town, t1recv.at[k], t1_send.at[k], t1_recv.at[k], quad_peers[k - 1])
-        copy.start()
-        t1_copies.append(copy)
-    pl.loop(4, 8)(lambda n: grad(1, n))
-    store_grads = pltpu.make_async_copy(grads, grads_out, l_sem.at[5])
-    store_grads.start()
-    for copy in t1_copies:
-        copy.wait_recv()
-    tbuf[z] = town[...] + t1recv[1] + t1recv[2] + t1recv[3]
+    for n in range(1, 32):
+        t1_copies[n - 1].wait_recv()
+        total = total + trecv[n]
+    tbuf[z] = total
     t2_copies = []
     for k in range(1, 16):
         copy = remote(tbuf.at[z], tbuf.at[z], t2_send.at[k], t2_recv.at[k], z_peers[k - 1])
@@ -347,7 +384,7 @@
         p_copies[k - 1].wait_recv()
         total = total + precv[k]
     proj_out[...] = total
-    for copy in q_copies + g_copies + sent + e_copies + e2_copies + p_copies + t0_copies + t1_copies:
+    for copy in q_copies + g_copies + sent + e_copies + e2_copies + p_copies + t1_copies:
         copy.wait_send()
     for copy in e2_copies:
         copy.wait_recv()
@@ -387,7 +424,7 @@
     embedding = frequency_embedding(timesteps, 256)
     vmem = pl.BlockSpec(memory_space=pltpu.VMEM)
     smem = pl.BlockSpec(memory_space=pltpu.SMEM)
-    anywhere = pl.BlockSpec(memory_space=pl.ANY)
+    anywhere = pl.BlockSpec(memory_space=pltpu.HBM)
     dma = pltpu.SemaphoreType.DMA
     count = OWN + 1
     mixed, grads, projected, gwg = pl.pallas_call(
@@ -398,14 +435,17 @@
             jax.ShapeDtypeStruct((8, 64), F32),
             jax.ShapeDtypeStruct((256, 256), F32),
         ),
-        in_specs=[vmem, vmem, smem, vmem, anywhere, anywhere, anywhere, anywhere],
+        in_specs=[vmem, vmem, smem, anywhere, anywhere, anywhere, anywhere, anywhere],
         out_specs=(anywhere, anywhere, vmem, vmem),
         scratch_shapes=[
             pltpu.VMEM((2048, 2048), BF16),
             pltpu.VMEM((192, 2048), BF16),
             pltpu.VMEM((192, 2048), BF16),
-            pltpu.VMEM((2048, 64), BF16),
-            pltpu.VMEM((2048, 64), BF16),
+            pltpu.VMEM((64, 2048), BF16),
+            pltpu.VMEM((64, 2048), BF16),
+            pltpu.VMEM((256, 256), BF16),
+            pltpu.VMEM((192, 2048), BF16),
+            pltpu.VMEM((128, 128), BF16),
             pltpu.VMEM((192, 2048), BF16),
             pltpu.VMEM((192, 2048), BF16),
             pltpu.VMEM((192, 2048), BF16),
@@ -418,21 +458,18 @@
             pltpu.VMEM((4, 8, 128), F32),
             pltpu.VMEM((16, 8, 128), F32),
             pltpu.VMEM((8, 8, 128), F32),
-            pltpu.VMEM((8, 8, 128), F32),
-            pltpu.VMEM((8, 128), F32),
-            pltpu.VMEM((4, 8, 128), F32),
+            pltpu.VMEM((32, 8, 128), F32),
             pltpu.VMEM((16, 8, 128), F32),
-            dma((6,)),
+            dma((7,)),
             dma((4,)), dma((4,)),
             dma((8,)), dma((8,)),
-            dma((H, 8)), dma((H, 8)),
+            dma((8,)), dma((8,)),
             dma((H, count)), dma((H, count)),
             dma((H, count)), dma((H, count)),
             dma((8,)), dma((8,)),
             dma((4,)), dma((4,)),
             dma((16,)), dma((16,)),
-            dma((8,)), dma((8,)),
-            dma((4,)), dma((4,)),
+            dma((32,)), dma((32,)),
             dma((16,)), dma((16,)),
         ],
         compiler_params=pltpu.CompilerParams(
@@ -443,7 +480,7 @@
         ),
     )(
         out_weight, embedding, text_lengths, gate_weight,
-        values[0], cotangent[0], in_probe, out_probe,
+        values[0], cotangent[0], in_probe.T, out_probe.T,
     )
     return mixed[None], grads[None], projected[None], gwg
 

time: 92.3 us -> 96.3 us (1.043)
  Pallas kernels: 82.8 us -> 84.7 us
  local copies, waits for them, and re-layouts: 6.54 us -> 8.12 us
    pallas_call x1, Pallas kernels: 82.8 us -> 84.7 us  [per_device(): pl.pallas_call(kernel, out_shape=(jax.ShapeDtypeStruct((192, 2048), BF16)...]
    unnamed x14 -> x16, local copies, waits for them, and re-layouts: 6.54 us -> 8.12 us
where the time goes in v2:
time: 96.3 us; the launch traced here: 94.9 us
  Pallas kernels  84.7 us (88%)
  local copies, waits for them, and re-layouts  8.12 us (8%)
  between operations  1.99 us (2%)
    pallas_call x1, Pallas kernels, per_device(): pl.pallas_call(kernel, out_shape=(jax.ShapeDtypeStruct((192, 2048), BF16)...  84.7 us
    unnamed x16, local copies, waits for them, and re-layouts  8.12 us

profile of v2, /device:TPU:6, one launch (start us, length us, event | category | flops | bytes accessed | tf_op | source)
XLA Modules:
  0.0 94.9 jit_solution(17443344388436516514)
XLA Ops:
  0.6 0.0 copy-start.5
  1.9 0.1 fusion
  2.0 0.0 copy-done.5
  2.0 0.0 copy-start
  2.0 1.1 %copy-done = bf16[1,192,2048]{2,1,0:T(8,128)(2,1)S(1)} copy-done((bf16[1,192,2048]{2,1,0:T(8,128)(2,1)S(1)}, bf16[1,192,2048]{2,1,0:T(8,128)(2,1)}, u32[]{:S(2)}) %copy-start) | copy-done | bytes 786456
  3.2 0.0 copy-start.1
  3.2 1.1 %copy-done.1 = bf16[1,192,2048]{2,1,0:T(8,128)(2,1)S(1)} copy-done((bf16[1,192,2048]{2,1,0:T(8,128)(2,1)S(1)}, bf16[1,192,2048]{2,1,0:T(8,128)(2,1)}, u32[]{:S(2)}) %copy-start.1) | copy-done | bytes 786456
  4.3 0.0 copy-start.2
  4.3 0.9 copy-done.2
  5.2 0.0 copy-start.3
  5.2 0.9 copy-done.3
  6.2 0.0 copy-start.4
  6.2 0.9 copy-done.4
  7.1 84.7 %shard_map.111 = (bf16[192,2048]{1,0:T(8,128)(2,1)S(1)}, bf16[192,2048]{1,0:T(8,128)(2,1)S(1)}, f32[8,64]{1,0:T(8,128)S(1)}, f32[256,256]{1,0:T(8,128)S(1)}) custom-call(bf16[4,2048]{1,0:T(4,128)(2,1)S(1)} %copy-done.5, f32[1,256]{1,0:T(1,128)S(1)} %pad_maximum_fusion.emb_ref, s32[1]{0:T(128)S(6)} %copy.17.len_ref, bf16[256,256]{1,0:T(8,128)(2,1)S(1)} %copy-done.4, ...), custom_call_target="tpu_custom_call" | custom-call | flops 3221225472 | bytes 3145728 | tf_op jit(solution)/shard_map/pallas_call | solution.py:430
  91.8 0.9 copy.18
  92.7 0.9 copy.19
  93.6 0.6 copy.20
  94.2 0.7 copy.21
  (1 shorter events, 0.0 us)
Async XLA Ops:
  0.6 1.4 %copy-start.5 = (bf16[4,2048]{1,0:T(4,128)(2,1)S(1)}, bf16[4,2048]{1,0:T(4,128)(2,1)}, u32[]{:S(2)}) copy-start(bf16[4,2048]{1,0:T(4,128)(2,1)} %w_ref.1) | copy-start | bytes 49156
  2.0 1.1 %copy-start = (bf16[1,192,2048]{2,1,0:T(8,128)(2,1)S(1)}, bf16[1,192,2048]{2,1,0:T(8,128)(2,1)}, u32[]{:S(2)}) copy-start(bf16[1,192,2048]{2,1,0:T(8,128)(2,1)} %param.8) | copy-start | bytes 2359300
  3.2 1.1 %copy-start.1 = (bf16[1,192,2048]{2,1,0:T(8,128)(2,1)S(1)}, bf16[1,192,2048]{2,1,0:T(8,128)(2,1)}, u32[]{:S(2)}) copy-start(bf16[1,192,2048]{2,1,0:T(8,128)(2,1)} %param.9) | copy-start | bytes 2359300
  4.3 0.9 %copy-start.2 = (bf16[2048,64]{0,1:T(8,128)(2,1)S(1)}, bf16[2048,64]{0,1:T(8,128)(2,1)}, u32[]{:S(2)}) copy-start(bf16[2048,64]{0,1:T(8,128)(2,1)} %param.12) | copy-start | bytes 786436
  5.2 0.9 %copy-start.3 = (bf16[2048,64]{0,1:T(8,128)(2,1)S(1)}, bf16[2048,64]{0,1:T(8,128)(2,1)}, u32[]{:S(2)}) copy-start(bf16[2048,64]{0,1:T(8,128)(2,1)} %param.13) | copy-start | bytes 786436
  6.2 0.9 copy-start.4

commit v3 on v2

--- a/solution.py
+++ b/solution.py
@@ -11,6 +11,8 @@
 GROUPS = ((0, 48), (48, 80))
 SLOTS = ((1, 2), (3, 4, 5, 6, 7))
 H = len(GROUPS)
+FAR_FIRST = (8, 7, 9, 6, 10, 5, 11, 4, 12, 3, 13, 2, 14, 1, 15)
+VMEM_BYTES = 63 * 1024 * 1024
 
 AXIS = [(-1, 0), (0, -1), (1, 0), (0, 1), (2, 0), (0, 2)]
 FORWARDED = [(i, -1, "A") for i in (-1, 1, 2)] + [(-1, j, "B") for j in (-1, 1, 2)]
@@ -48,10 +50,10 @@
 def kernel(
     w_ref, emb_ref, len_ref, gw_ref, values_ref, cot_ref, inp_ref, outp_ref,
     mixed_out, grads_out, proj_out, gwg_out,
-    wbuf, vals, cot, inp, outp, gw, valsp, place, masked, mixed, grads, acc, gate,
+    wbuf, vals, cot, inp, outp, gw, valsp, place, masked, mixed, grads, gradsp, left, acc, gate,
     qbuf, psend, precv, eown, erecv, ebuf, tsend, trecv, tbuf,
     l_sem, q_send, q_recv, g_send, g_recv, z_send, z_recv, x_send, x_recv, d_send, d_recv,
-    p_send, p_recv, e1_send, e1_recv, e2_send, e2_recv, t1_send, t1_recv, t2_send, t2_recv,
+    far_sem, p_send, p_recv, e1_send, e1_recv, e2_send, e2_recv, t1_send, t1_recv, t2_send, t2_recv,
 ):
     f, d = lax.axis_index("fsdp"), lax.axis_index("dp")
     x_lo, y = f // 4, f % 4
@@ -94,7 +96,7 @@
     }
 
     barrier = pltpu.get_barrier_semaphore()
-    greeted = z_peers + f_peers + quad_peers
+    greeted = [z_peers[k - 1] for k in (4, 12, 3, 13, 2, 14, 1, 15)] + f_peers + quad_peers
     greeted = greeted + [
         (f, x_hi * 32 + (z + 1 - 2 * p) * 2 + 1 - c),
         ((1 - x_lo) * 4 + y, (1 - x_hi) * 32 + z * 2 + c),
@@ -108,6 +110,8 @@
         [mine[:, 512 * n : 512 * n + 512] for n in range(4)], axis=0
     ).astype(BF16)
     pl.semaphore_wait(barrier, len(greeted))
+    for k in (4, 12):
+        pl.semaphore_signal(far_sem, inc=1, device_id=z_peers[k - 1], device_id_type=MESH)
 
     q_copies = []
     for k in range(1, 4):
@@ -160,6 +164,8 @@
 
     sent = []
     for k in range(1, 8):
+        if k == 5:
+            pl.semaphore_wait(far_sem, 2)
         away = (k + 1) // 2
         slot = 2 * away - 1 + (p if away < 4 else 0)
         there = pl.ds(pl.multiple_of(own + 16 * slot, 16), 16)
@@ -229,13 +235,25 @@
         copy.start()
         e_copies.append(copy)
 
+    k_at = lax.broadcasted_iota(jnp.int32, (128, 128), 0)
+    n_at = lax.broadcasted_iota(jnp.int32, (128, 128), 1)
+    slot_at = n_at // 16
+    away_at = jnp.where(slot_at % 2 == 1, (slot_at + 1) // 2, 8 - slot_at // 2)
+    place[...] = jnp.where(k_at == (m + away_at) % 8 * 16 + n_at % 16, 1.0, 0.0).astype(BF16)
+
+    for load in loads[1:]:
+        load.wait()
+    for n in range(16):
+        cols = slice(128 * n, 128 * n + 128)
+        valsp[:, cols] = jnp.dot(
+            vals[:, cols], place[...], preferred_element_type=F32
+        ).astype(BF16)
+
     z_wait(0)
     forward(0, (0, 0, "AB"))
 
     for copy in g_copies:
         copy.wait_recv()
-    for load in loads[1:]:
-        load.wait()
     limit = 8 * 192 - TXT + len_ref[0]
 
     def valid(width):
@@ -246,19 +264,6 @@
         cols = pl.ds(pl.multiple_of(n * 256, 256), 256)
         scaled = jnp.where(valid(256), cot[:, cols].astype(F32), 0.0)
         masked[:, cols] = (scaled * gate[0:1, cols]).astype(BF16)
-
-    k_at = lax.broadcasted_iota(jnp.int32, (128, 128), 0)
-    n_at = lax.broadcasted_iota(jnp.int32, (128, 128), 1)
-    slot_at = n_at // 16
-    away_at = jnp.where(slot_at % 2 == 1, (slot_at + 1) // 2, 8 - slot_at // 2)
-    place[...] = jnp.where(k_at == (m + away_at) % 8 * 16 + n_at % 16, 1.0, 0.0).astype(BF16)
-
-    @pl.loop(0, 16)
-    def _(n):
-        cols = pl.ds(pl.multiple_of(n * 128, 128), 128)
-        valsp[:, cols] = jnp.dot(
-            vals[:, cols], place[...], preferred_element_type=F32
-        ).astype(BF16)
 
     for i, j in AXIS:
         take(0, (i, j, "AB"))
@@ -271,7 +276,7 @@
         copy.wait_recv()
     ebuf[z] = eown[...] + erecv[1] + erecv[2] + erecv[3]
     e2_copies = []
-    for k in range(1, 16):
+    for k in FAR_FIRST:
         copy = remote(ebuf.at[z], ebuf.at[z], e2_send.at[k], e2_recv.at[k], z_peers[k - 1])
         copy.start()
         e2_copies.append(copy)
@@ -302,22 +307,14 @@
     def branch(i, j, first=False):
         rows = pair_rows(i, j)
 
-        @pl.loop(0, 8)
-        def _(n):
-            cols = pl.ds(pl.multiple_of(n * 256, 256), 256)
-            product = jnp.dot(valsp[:, rows], wbuf[rows, cols], preferred_element_type=F32)
-            acc[:, cols] = product if first else acc[:, cols] + product
+        product = jnp.dot(valsp[:, rows], wbuf[rows, :], preferred_element_type=F32)
+        acc[...] = product if first else acc[...] + product
 
     def grad(i, j):
         rows = pair_rows(i, j)
-        slots = lax.dot_general(
+        gradsp[:, rows] = lax.dot_general(
             masked[...], wbuf[rows, :], turned, preferred_element_type=F32
         ).astype(BF16)
-        for n in range(2):
-            cols = pl.ds(pl.multiple_of(rows.start + 128 * n, 128), 128)
-            grads[:, cols] = lax.dot_general(
-                slots[:, 128 * n : 128 * n + 128], place[...], turned, preferred_element_type=F32
-            ).astype(BF16)
 
     def pair_wait(i, j):
         for i_each in (0, 2) if i == 0 else (-1, 1):
@@ -331,81 +328,84 @@
     branch(1, 0)
     for message in SIDE:
         take(1, message)
-    grad(0, 0)
-    grad(1, 0)
     for j in (-1, 1):
         pair_wait(1, j)
         branch(1, j)
-        grad(1, j)
+    grad(0, 0)
+    grad(1, 0)
     for message in LAST:
         take(1, message)
     for i, j in ((0, -1), (0, 1), (1, 2), (0, 2)):
         pair_wait(i, j)
         branch(i, j)
 
-    @pl.loop(0, 8)
-    def _(n):
-        cols = pl.ds(pl.multiple_of(n * 256, 256), 256)
-        product = acc[:, cols]
+    for n in range(8):
+        cols = slice(256 * n, 256 * n + 256)
         scaled = jnp.where(valid(256), cot[:, cols].astype(F32), 0.0)
-        tsend[n] = tile_of(jnp.sum(scaled * product, axis=0, keepdims=True))
-        mixed[:, cols] = (product * gate[0:1, cols]).astype(BF16)
-
-    t1_copies = []
-    for k in range(8):
-        to_f = (f + k) % 8
-        for k_quad in range(4):
-            n = 4 * k + k_quad
-            if n:
-                t = (e + k_quad) % 4
-                target = (to_f, (t // 2) * 32 + z * 2 + t % 2)
-                copy = remote(tsend.at[to_f], trecv.at[n], t1_send.at[n], t1_recv.at[n], target)
-                copy.start()
-                t1_copies.append(copy)
+        tsend[n] = tile_of(jnp.sum(scaled * acc[:, cols], axis=0, keepdims=True))
+
+    t1_copies = {}
+    for n in sorted(range(1, 32), key=lambda n: -(n // 4 in (2, 6)) - (n % 4 in (1, 2, 3))):
+        to_f, t = (f + n // 4) % 8, (e + n % 4) % 4
+        copy = remote(
+            tsend.at[to_f], trecv.at[n], t1_send.at[n], t1_recv.at[n],
+            (to_f, (t // 2) * 32 + z * 2 + t % 2),
+        )
+        copy.start()
+        t1_copies[n] = copy
+    for n in range(8):
+        cols = slice(256 * n, 256 * n + 256)
+        mixed[:, cols] = (acc[:, cols] * gate[0:1, cols]).astype(BF16)
     store_mixed = pltpu.make_async_copy(mixed, mixed_out, l_sem.at[5])
     store_mixed.start()
-    for i, j in ((0, -1), (0, 1), (1, 2), (0, 2)):
+    for i, j in ((1, -1), (1, 1), (0, -1)):
         grad(i, j)
-    store_grads = pltpu.make_async_copy(grads, grads_out, l_sem.at[6])
-    store_grads.start()
     total = tsend[f]
     for n in range(1, 32):
-        t1_copies[n - 1].wait_recv()
+        t1_copies[n].wait_recv()
         total = total + trecv[n]
     tbuf[z] = total
     t2_copies = []
-    for k in range(1, 16):
+    for k in FAR_FIRST:
         copy = remote(tbuf.at[z], tbuf.at[z], t2_send.at[k], t2_recv.at[k], z_peers[k - 1])
         copy.start()
         t2_copies.append(copy)
+    for i, j in ((0, 1), (1, 2), (0, 2)):
+        grad(i, j)
+    for n in range(16):
+        cols = slice(128 * n, 128 * n + 128)
+        grads[:, cols] = lax.dot_general(
+            gradsp[:, cols], place[...], turned, preferred_element_type=F32
+        ).astype(BF16)
+    store_grads = pltpu.make_async_copy(grads, grads_out, l_sem.at[6])
+    store_grads.start()
+
+    for copy in e2_copies:
+        copy.wait_recv()
+    emb_all = ebuf[...].reshape(128, 128) * (8 * 192 * 64) ** (-0.5)
+    in_high = lax.broadcasted_iota(jnp.int32, (128, 128), 0) % 8 >= 4
+    for half in range(2):
+        for k_half in range(2):
+            rows = emb_all
+            if k_half != half:
+                rows = pltpu.roll(emb_all, 4 if half else 124, 0)
+            rows = jnp.where(in_high if half else jnp.logical_not(in_high), rows, 0.0)
+            left[half, 128 * k_half : 128 * k_half + 128, :] = rows.T
 
     total = psend[f]
     for k in range(1, 8):
         p_copies[k - 1].wait_recv()
         total = total + precv[k]
     proj_out[...] = total
-    for copy in q_copies + g_copies + sent + e_copies + e2_copies + p_copies + t1_copies:
+    for copy in q_copies + g_copies + sent + e_copies + e2_copies + p_copies + list(t1_copies.values()):
         copy.wait_send()
-    for copy in e2_copies:
-        copy.wait_recv()
     for copy in t2_copies:
         copy.wait()
-
-    emb_all = ebuf[...].reshape(128, 128)
     grad_all = tbuf[...].reshape(128, 128)
-    in_high = lax.broadcasted_iota(jnp.int32, (128, 128), 0) % 8 >= 4
     for half in range(2):
-        ours = jnp.where(in_high if half else jnp.logical_not(in_high), grad_all, 0.0)
-        for k_half in range(2):
-            rows = emb_all
-            if k_half != half:
-                rows = pltpu.roll(emb_all, 4 if half else 124, 0)
-            gwg_out[128 * k_half : 128 * k_half + 128, 128 * half : 128 * half + 128] = (
-                lax.dot_general(
-                    rows, ours, (((0,), (0,)), ((), ())),
-                    precision=lax.Precision.HIGHEST, preferred_element_type=F32,
-                ) * (8 * 192 * 64) ** (-0.5)
-            )
+        gwg_out[:, 128 * half : 128 * half + 128] = jnp.dot(
+            left[half], grad_all, precision=lax.Precision.HIGHEST, preferred_element_type=F32
+        )
     store_mixed.wait()
     store_grads.wait()
 
@@ -449,6 +449,8 @@
             pltpu.VMEM((192, 2048), BF16),
             pltpu.VMEM((192, 2048), BF16),
             pltpu.VMEM((192, 2048), BF16),
+            pltpu.VMEM((192, 2048), BF16),
+            pltpu.VMEM((2, 256, 128), F32),
             pltpu.VMEM((192, 2048), F32),
             pltpu.VMEM((8, 2048), F32),
             pltpu.VMEM((4, 16, 512), BF16),
@@ -466,6 +468,7 @@
             dma((8,)), dma((8,)),
             dma((H, count)), dma((H, count)),
             dma((H, count)), dma((H, count)),
+            pltpu.SemaphoreType.REGULAR,
             dma((8,)), dma((8,)),
             dma((4,)), dma((4,)),
             dma((16,)), dma((16,)),
@@ -473,7 +476,7 @@
             dma((16,)), dma((16,)),
         ],
         compiler_params=pltpu.CompilerParams(
-            collective_id=0, has_side_effects=True, vmem_limit_bytes=40 * 1024 * 1024
+            collective_id=0, has_side_effects=True, vmem_limit_bytes=VMEM_BYTES
         ),
         cost_estimate=pl.CostEstimate(
             flops=4 * 192 * 2048 * 2048, bytes_accessed=8 * 192 * 2048, transcendentals=0

time: 96.3 us -> 78.1 us (0.81)
  Pallas kernels: 84.7 us -> 70.5 us
  local copies, waits for them, and re-layouts: 8.12 us -> 4.35 us
    pallas_call x1, Pallas kernels: 84.7 us -> 70.5 us  [per_device(): pl.pallas_call(kernel, out_shape=(jax.ShapeDtypeStruct((192, 2048), BF16)...]
    unnamed x16 -> x10, local copies, waits for them, and re-layouts: 8.12 us -> 4.35 us
where the time goes in v3:
time: 78.1 us; the launch traced here: 77.4 us
  Pallas kernels  70.5 us (90%)
  local copies, waits for them, and re-layouts  4.35 us (6%)
  between operations  1.95 us (2%)
    pallas_call x1, Pallas kernels, per_device(): pl.pallas_call(kernel, out_shape=(jax.ShapeDtypeStruct((192, 2048), BF16)...  70.5 us
    unnamed x10, local copies, waits for them, and re-layouts  4.35 us

profile of v3, /device:TPU:6, one launch (start us, length us, event | category | flops | bytes accessed | tf_op | source)
XLA Modules:
  0.0 77.4 jit_solution(14658172983900757631)
XLA Ops:
  1.9 0.1 fusion
  2.0 0.6 pad_maximum_fusion.emb_ref
  2.6 70.5 %shard_map.111 = (bf16[192,2048]{1,0:T(8,128)(2,1)}, bf16[192,2048]{1,0:T(8,128)(2,1)}, f32[8,64]{1,0:T(8,128)}, f32[256,256]{1,0:T(8,128)}) custom-call(bf16[4,2048]{1,0:T(4,128)(2,1)} %w_ref.1, f32[1,256]{1,0:T(1,128)} %pad_maximum_fusion.emb_ref, s32[1]{0:T(128)S(6)} %copy.17.len_ref, bf16[256,256]{1,0:T(8,128)(2,1)} %gw_ref.1, ...), custom_call_target="tpu_custom_call" | custom-call | flops 3221225472 | bytes 3145728 | tf_op jit(solution)/shard_map/pallas_call | solution.py:430
  73.0 0.0 copy-start
  73.0 2.2 %copy.18 = bf16[1,192,2048]{2,1,0:T(8,128)(2,1)} copy(bf16[1,192,2048]{2,1,0:T(8,128)(2,1)} %bitcast.9) | data formatting | bytes 1572864
  75.2 0.0 copy-done
  75.2 0.0 copy-start.2
  75.2 0.0 copy-start.1
  75.2 0.9 %copy.19 = bf16[1,192,2048]{2,1,0:T(8,128)(2,1)} copy(bf16[1,192,2048]{2,1,0:T(8,128)(2,1)S(1)} %bitcast.8) | data formatting | bytes 1572864
  76.1 0.0 copy-done.2
  76.1 0.6 copy.20
  76.7 0.0 copy-done.1
  76.7 0.7 copy.21
Async XLA Ops:
  73.0 2.2 %copy-start = (bf16[192,2048]{1,0:T(8,128)(2,1)S(1)}, bf16[192,2048]{1,0:T(8,128)(2,1)}, u32[]{:S(2)}) copy-start(bf16[192,2048]{1,0:T(8,128)(2,1)} %get-tuple-element.9) | copy-start | bytes 2359300
  75.2 0.9 %copy-start.2 = (f32[8,64]{1,0:T(8,128)S(1)}, f32[8,64]{1,0:T(8,128)}, u32[]{:S(2)}) copy-start(f32[8,64]{1,0:T(8,128)} %get-tuple-element.10) | copy-start | bytes 6148
  75.2 1.5 %copy-start.1 = (f32[256,256]{1,0:T(8,128)S(1)}, f32[256,256]{1,0:T(8,128)}, u32[]{:S(2)}) copy-start(f32[256,256]{1,0:T(8,128)} %get-tuple-element.21) | copy-start | bytes 786436

commit v4 on v3

--- a/solution.py
+++ b/solution.py
@@ -8,8 +8,7 @@
 MESH = pl.DeviceIdType.MESH
 F32, BF16 = jnp.float32, jnp.bfloat16
 TXT = 256
-GROUPS = ((0, 48), (48, 80))
-SLOTS = ((1, 2), (3, 4, 5, 6, 7))
+GROUPS = ((0, 16), (16, 32), (48, 80))
 H = len(GROUPS)
 FAR_FIRST = (8, 7, 9, 6, 10, 5, 11, 4, 12, 3, 13, 2, 14, 1, 15)
 VMEM_BYTES = 63 * 1024 * 1024
@@ -53,7 +52,7 @@
     wbuf, vals, cot, inp, outp, gw, valsp, place, masked, mixed, grads, gradsp, left, acc, gate,
     qbuf, psend, precv, eown, erecv, ebuf, tsend, trecv, tbuf,
     l_sem, q_send, q_recv, g_send, g_recv, z_send, z_recv, x_send, x_recv, d_send, d_recv,
-    far_sem, p_send, p_recv, e1_send, e1_recv, e2_send, e2_recv, t1_send, t1_recv, t2_send, t2_recv,
+    p_send, p_recv, e1_send, e1_recv, e2_send, e2_recv, t1_send, t1_recv, t2_send, t2_recv,
 ):
     f, d = lax.axis_index("fsdp"), lax.axis_index("dp")
     x_lo, y = f // 4, f % 4
@@ -110,8 +109,6 @@
         [mine[:, 512 * n : 512 * n + 512] for n in range(4)], axis=0
     ).astype(BF16)
     pl.semaphore_wait(barrier, len(greeted))
-    for k in (4, 12):
-        pl.semaphore_signal(far_sem, inc=1, device_id=z_peers[k - 1], device_id_type=MESH)
 
     q_copies = []
     for k in range(1, 4):
@@ -163,23 +160,27 @@
     wbuf[own_rows, half_cols] = jnp.where(c == 0, low, high).astype(BF16)
 
     sent = []
-    for k in range(1, 8):
-        if k == 5:
-            pl.semaphore_wait(far_sem, 2)
+
+    def z_rows(slot):
+        return pl.ds(pl.multiple_of(own + 16 * slot, 16), 16)
+
+    def z_copy(k):
         away = (k + 1) // 2
         slot = 2 * away - 1 + (p if away < 4 else 0)
-        there = pl.ds(pl.multiple_of(own + 16 * slot, 16), 16)
+        source, hops = (own_rows, k) if k <= 4 else (z_rows(3 + p), k - 4)
         copy = remote(
-            wbuf.at[own_rows, half_cols], wbuf.at[there, half_cols], z_send.at[k], z_recv.at[slot],
-            device(x, y, (z + (2 * p - 1) * k + 16) % 16, c),
+            wbuf.at[source, half_cols], wbuf.at[z_rows(slot), half_cols], z_send.at[k],
+            z_recv.at[slot], device(x, y, (z + (2 * p - 1) * hops + 16) % 16, c),
         )
         copy.start()
         sent.append(copy)
 
-    def z_wait(h):
-        for slot in SLOTS[h]:
-            block = wbuf.at[pl.ds(pl.multiple_of(own + 16 * slot, 16), 16), half_cols]
-            remote(block, block, z_send.at[slot], z_recv.at[slot], core_peer).wait_recv()
+    def z_wait(slot):
+        block = wbuf.at[z_rows(slot), half_cols]
+        remote(block, block, z_send.at[slot], z_recv.at[slot], core_peer).wait_recv()
+
+    for k in (4, 1, 2, 3):
+        z_copy(k)
 
     def block_of(core, h, message):
         i, j, part = message
@@ -219,6 +220,7 @@
                 block = block_of(1 - c, h, (i, j, part))
                 remote(block, block, d_send.at[h, n], d_recv.at[h, n], core_peer).wait_recv()
 
+    forward(0, (0, 0, "AB"))
     e = 2 * x_hi + c
     tile_row = lax.broadcasted_iota(jnp.int32, (8, 128), 0)
 
@@ -249,8 +251,12 @@
             vals[:, cols], place[...], preferred_element_type=F32
         ).astype(BF16)
 
-    z_wait(0)
-    forward(0, (0, 0, "AB"))
+    for slot in (1, 2):
+        z_wait(slot)
+    forward(1, (0, 0, "AB"))
+    z_wait(3 + p)
+    for k in (7, 6, 5):
+        z_copy(k)
 
     for copy in g_copies:
         copy.wait_recv()
@@ -265,12 +271,15 @@
         scaled = jnp.where(valid(256), cot[:, cols].astype(F32), 0.0)
         masked[:, cols] = (scaled * gate[0:1, cols]).astype(BF16)
 
-    for i, j in AXIS:
-        take(0, (i, j, "AB"))
-    z_wait(1)
-    forward(1, (0, 0, "AB"))
-    for message in FORWARDED:
-        take(0, message)
+    for h in range(2):
+        for i, j in AXIS:
+            take(h, (i, j, "AB"))
+    for slot in (4 - p, 5, 6, 7):
+        z_wait(slot)
+    forward(2, (0, 0, "AB"))
+    for h in range(2):
+        for message in FORWARDED:
+            take(h, message)
 
     for copy in e_copies:
         copy.wait_recv()
@@ -282,7 +291,7 @@
         e2_copies.append(copy)
 
     for i, j in AXIS:
-        take(1, (i, j, "AB"))
+        take(2, (i, j, "AB"))
 
     turned = (((1,), (1,)), ((), ()))
     probe_in = lax.dot_general(vals[...], inp[...], turned, preferred_element_type=F32).astype(BF16)
@@ -297,8 +306,9 @@
         copy.start()
         p_copies.append(copy)
 
-    for message in FINAL:
-        take(0, message)
+    for h in range(2):
+        for message in FINAL:
+            take(h, message)
 
     def pair_rows(i, j):
         xx, yy = (x + i + 8) % 2, (y + s * j + 8) % 4
@@ -321,20 +331,20 @@
             from_other_core(i_each, j)
 
     for message in FORWARDED:
-        take(1, message)
+        take(2, message)
     pair_wait(0, 0)
     branch(0, 0, first=True)
     pair_wait(1, 0)
     branch(1, 0)
     for message in SIDE:
-        take(1, message)
+        take(2, message)
     for j in (-1, 1):
         pair_wait(1, j)
         branch(1, j)
     grad(0, 0)
     grad(1, 0)
     for message in LAST:
-        take(1, message)
+        take(2, message)
     for i, j in ((0, -1), (0, 1), (1, 2), (0, 2)):
         pair_wait(i, j)
         branch(i, j)
@@ -468,7 +478,6 @@
             dma((8,)), dma((8,)),
             dma((H, count)), dma((H, count)),
             dma((H, count)), dma((H, count)),
-            pltpu.SemaphoreType.REGULAR,
             dma((8,)), dma((8,)),
             dma((4,)), dma((4,)),
             dma((16,)), dma((16,)),

time: 78.1 us -> 79.1 us (1.013)
  no operation moved by 1% of the time
where the time goes in v4:
time: 79.1 us; the launch traced here: 78.1 us
  Pallas kernels  71.2 us (90%)
  local copies, waits for them, and re-layouts  4.35 us (5%)
  between operations  1.95 us (2%)
    pallas_call x1, Pallas kernels, per_device(): pl.pallas_call(kernel, out_shape=(jax.ShapeDtypeStruct((192, 2048), BF16)...  71.2 us
    unnamed x10, local copies, waits for them, and re-layouts  4.35 us

profile of v4, /device:TPU:6, one launch (start us, length us, event | category | flops | bytes accessed | tf_op | source)
XLA Modules:
  0.0 78.1 jit_solution(13892258021843903744)
XLA Ops:
  1.9 0.1 fusion
  2.0 0.6 pad_maximum_fusion.emb_ref
  2.6 71.2 %shard_map.111 = (bf16[192,2048]{1,0:T(8,128)(2,1)}, bf16[192,2048]{1,0:T(8,128)(2,1)}, f32[8,64]{1,0:T(8,128)}, f32[256,256]{1,0:T(8,128)}) custom-call(bf16[4,2048]{1,0:T(4,128)(2,1)} %w_ref.1, f32[1,256]{1,0:T(1,128)} %pad_maximum_fusion.emb_ref, s32[1]{0:T(128)S(6)} %copy.17.len_ref, bf16[256,256]{1,0:T(8,128)(2,1)} %gw_ref.1, ...), custom_call_target="tpu_custom_call" | custom-call | flops 3221225472 | bytes 3145728 | tf_op jit(solution)/shard_map/pallas_call | solution.py:440
  73.8 0.0 copy-start
  73.8 2.2 %copy.18 = bf16[1,192,2048]{2,1,0:T(8,128)(2,1)} copy(bf16[1,192,2048]{2,1,0:T(8,128)(2,1)} %bitcast.9) | data formatting | bytes 1572864
  76.0 0.0 copy-done
  76.0 0.0 copy-start.2
  76.0 0.0 copy-start.1
  76.0 0.9 %copy.19 = bf16[1,192,2048]{2,1,0:T(8,128)(2,1)} copy(bf16[1,192,2048]{2,1,0:T(8,128)(2,1)S(1)} %bitcast.8) | data formatting | bytes 1572864
  76.8 0.0 copy-done.2
  76.8 0.6 copy.20
  77.4 0.0 copy-done.1
  77.4 0.7 copy.21
Async XLA Ops:
  73.8 2.2 %copy-start = (bf16[192,2048]{1,0:T(8,128)(2,1)S(1)}, bf16[192,2048]{1,0:T(8,128)(2,1)}, u32[]{:S(2)}) copy-start(bf16[192,2048]{1,0:T(8,128)(2,1)} %get-tuple-element.9) | copy-start | bytes 2359300
  76.0 0.9 %copy-start.2 = (f32[8,64]{1,0:T(8,128)S(1)}, f32[8,64]{1,0:T(8,128)}, u32[]{:S(2)}) copy-start(f32[8,64]{1,0:T(8,128)} %get-tuple-element.10) | copy-start | bytes 6148
  76.0 1.5 %copy-start.1 = (f32[256,256]{1,0:T(8,128)S(1)}, f32[256,256]{1,0:T(8,128)}, u32[]{:S(2)}) copy-start(f32[256,256]{1,0:T(8,128)} %get-tuple-element.21) | copy-start | bytes 786436

commit v5 on v4

--- a/solution.py
+++ b/solution.py
@@ -8,7 +8,8 @@
 MESH = pl.DeviceIdType.MESH
 F32, BF16 = jnp.float32, jnp.bfloat16
 TXT = 256
-GROUPS = ((0, 16), (16, 32), (48, 80))
+GROUPS = ((0, 128),)
+PIECES = ((0, 48), (48, 80))
 H = len(GROUPS)
 FAR_FIRST = (8, 7, 9, 6, 10, 5, 11, 4, 12, 3, 13, 2, 14, 1, 15)
 VMEM_BYTES = 63 * 1024 * 1024
@@ -51,7 +52,7 @@
     mixed_out, grads_out, proj_out, gwg_out,
     wbuf, vals, cot, inp, outp, gw, valsp, place, masked, mixed, grads, gradsp, left, acc, gate,
     qbuf, psend, precv, eown, erecv, ebuf, tsend, trecv, tbuf,
-    l_sem, q_send, q_recv, g_send, g_recv, z_send, z_recv, x_send, x_recv, d_send, d_recv,
+    l_sem, q_send, q_recv, g_send, g_recv, z_send, z_recv, x_send, x_recv, d_send, d_recv, o_send, o_recv,
     p_send, p_recv, e1_send, e1_recv, e2_send, e2_recv, t1_send, t1_recv, t2_send, t2_recv,
 ):
     f, d = lax.axis_index("fsdp"), lax.axis_index("dp")
@@ -189,12 +190,21 @@
         return wbuf.at[rows, cols_of(core, part)]
 
 
+    def own_piece(piece):
+        first, count = PIECES[piece]
+        block = wbuf.at[pl.ds(pl.multiple_of(own + first, 16), count), half_cols]
+        for direction, there in onward((0, 0, "AB")):
+            n = INDEX[there]
+            copy = remote(block, block, o_send.at[piece, n], o_recv.at[piece, n], way[direction])
+            copy.start()
+            sent.append(copy)
+
     def part_block(h, message, part):
         return block_of(c, h, (message[0], message[1], part))
 
     def forward(h, message):
         i, j, part = message
-        for direction, there in onward(message):
+        for direction, there in onward(message) if (i, j) != (0, 0) else ():
             n = INDEX[there]
             block = part_block(h, message, there[2])
             copy = remote(block, block, x_send.at[h, n], x_recv.at[h, n], way[direction])
@@ -208,8 +218,14 @@
 
     def take(h, message):
         n = INDEX[message]
-        block = block_of(c, h, message)
-        remote(block, block, x_send.at[h, n], x_recv.at[h, n], core_peer).wait_recv()
+        if n < 4:
+            for piece, (first, count) in enumerate(PIECES):
+                rows = pl.ds(pl.multiple_of(row_of(*message[:2]) + first, 16), count)
+                block = wbuf.at[rows, half_cols]
+                remote(block, block, o_send.at[piece, n], o_recv.at[piece, n], core_peer).wait_recv()
+        else:
+            block = block_of(c, h, message)
+            remote(block, block, x_send.at[h, n], x_recv.at[h, n], core_peer).wait_recv()
         forward(h, message)
 
     def from_other_core(i, j):
@@ -220,7 +236,6 @@
                 block = block_of(1 - c, h, (i, j, part))
                 remote(block, block, d_send.at[h, n], d_recv.at[h, n], core_peer).wait_recv()
 
-    forward(0, (0, 0, "AB"))
     e = 2 * x_hi + c
     tile_row = lax.broadcasted_iota(jnp.int32, (8, 128), 0)
 
@@ -253,7 +268,7 @@
 
     for slot in (1, 2):
         z_wait(slot)
-    forward(1, (0, 0, "AB"))
+    own_piece(0)
     z_wait(3 + p)
     for k in (7, 6, 5):
         z_copy(k)
@@ -271,15 +286,12 @@
         scaled = jnp.where(valid(256), cot[:, cols].astype(F32), 0.0)
         masked[:, cols] = (scaled * gate[0:1, cols]).astype(BF16)
 
-    for h in range(2):
-        for i, j in AXIS:
-            take(h, (i, j, "AB"))
     for slot in (4 - p, 5, 6, 7):
         z_wait(slot)
-    forward(2, (0, 0, "AB"))
-    for h in range(2):
-        for message in FORWARDED:
-            take(h, message)
+    own_piece(1)
+    forward(0, (0, 0, "AB"))
+    for i, j in AXIS:
+        take(0, (i, j, "AB"))
 
     for copy in e_copies:
         copy.wait_recv()
@@ -291,7 +303,7 @@
         e2_copies.append(copy)
 
     for i, j in AXIS:
-        take(2, (i, j, "AB"))
+        pass
 
     turned = (((1,), (1,)), ((), ()))
     probe_in = lax.dot_general(vals[...], inp[...], turned, preferred_element_type=F32).astype(BF16)
@@ -306,9 +318,6 @@
         copy.start()
         p_copies.append(copy)
 
-    for h in range(2):
-        for message in FINAL:
-            take(h, message)
 
     def pair_rows(i, j):
         xx, yy = (x + i + 8) % 2, (y + s * j + 8) % 4
@@ -331,20 +340,20 @@
             from_other_core(i_each, j)
 
     for message in FORWARDED:
-        take(2, message)
+        take(0, message)
     pair_wait(0, 0)
     branch(0, 0, first=True)
     pair_wait(1, 0)
     branch(1, 0)
     for message in SIDE:
-        take(2, message)
+        take(0, message)
     for j in (-1, 1):
         pair_wait(1, j)
         branch(1, j)
     grad(0, 0)
     grad(1, 0)
     for message in LAST:
-        take(2, message)
+        take(0, message)
     for i, j in ((0, -1), (0, 1), (1, 2), (0, 2)):
         pair_wait(i, j)
         branch(i, j)
@@ -478,6 +487,7 @@
             dma((8,)), dma((8,)),
             dma((H, count)), dma((H, count)),
             dma((H, count)), dma((H, count)),
+            dma((2, 4)), dma((2, 4)),
             dma((8,)), dma((8,)),
             dma((4,)), dma((4,)),
             dma((16,)), dma((16,)),

time: 79.1 us -> 75.2 us (0.951)
  Pallas kernels: 71.2 us -> 68 us
    pallas_call x1, Pallas kernels: 71.2 us -> 68 us  [per_device(): pl.pallas_call(kernel, out_shape=(jax.ShapeDtypeStruct((192, 2048), BF16)...]
where the time goes in v5:
time: 75.2 us; the launch traced here: 75 us
  Pallas kernels  68 us (90%)
  local copies, waits for them, and re-layouts  4.35 us (6%)
  between operations  1.95 us (3%)
    pallas_call x1, Pallas kernels, per_device(): pl.pallas_call(kernel, out_shape=(jax.ShapeDtypeStruct((192, 2048), BF16)...  68 us
    unnamed x10, local copies, waits for them, and re-layouts  4.35 us

profile of v5, /device:TPU:6, one launch (start us, length us, event | category | flops | bytes accessed | tf_op | source)
XLA Modules:
  0.0 75.0 jit_solution(5729351951430806870)
XLA Ops:
  1.9 0.1 fusion
  2.0 0.6 pad_maximum_fusion.emb_ref
  2.6 68.0 %shard_map.111 = (bf16[192,2048]{1,0:T(8,128)(2,1)}, bf16[192,2048]{1,0:T(8,128)(2,1)}, f32[8,64]{1,0:T(8,128)}, f32[256,256]{1,0:T(8,128)}) custom-call(bf16[4,2048]{1,0:T(4,128)(2,1)} %w_ref.1, f32[1,256]{1,0:T(1,128)} %pad_maximum_fusion.emb_ref, s32[1]{0:T(128)S(6)} %copy.17.len_ref, bf16[256,256]{1,0:T(8,128)(2,1)} %gw_ref.1, ...), custom_call_target="tpu_custom_call" | custom-call | flops 3221225472 | bytes 3145728 | tf_op jit(solution)/shard_map/pallas_call | solution.py:449
  70.6 0.0 copy-start
  70.6 2.2 %copy.18 = bf16[1,192,2048]{2,1,0:T(8,128)(2,1)} copy(bf16[1,192,2048]{2,1,0:T(8,128)(2,1)} %bitcast.9) | data formatting | bytes 1572864
  72.8 0.0 copy-done
  72.8 0.0 copy-start.2
  72.8 0.0 copy-start.1
  72.8 0.9 %copy.19 = bf16[1,192,2048]{2,1,0:T(8,128)(2,1)} copy(bf16[1,192,2048]{2,1,0:T(8,128)(2,1)S(1)} %bitcast.8) | data formatting | bytes 1572864
  73.7 0.0 copy-done.2
  73.7 0.6 copy.20
  74.2 0.0 copy-done.1
  74.2 0.7 copy.21
Async XLA Ops:
  70.6 2.2 %copy-start = (bf16[192,2048]{1,0:T(8,128)(2,1)S(1)}, bf16[192,2048]{1,0:T(8,128)(2,1)}, u32[]{:S(2)}) copy-start(bf16[192,2048]{1,0:T(8,128)(2,1)} %get-tuple-element.9) | copy-start | bytes 2359300
  72.8 0.9 %copy-start.2 = (f32[8,64]{1,0:T(8,128)S(1)}, f32[8,64]{1,0:T(8,128)}, u32[]{:S(2)}) copy-start(f32[8,64]{1,0:T(8,128)} %get-tuple-element.10) | copy-start | bytes 6148
  72.8 1.5 %copy-start.1 = (f32[256,256]{1,0:T(8,128)S(1)}, f32[256,256]{1,0:T(8,128)}, u32[]{:S(2)}) copy-start(f32[256,256]{1,0:T(8,128)} %get-tuple-element.21) | copy-start | bytes 786436

commit v6 on v5

--- a/solution.py
+++ b/solution.py
@@ -11,6 +11,7 @@
 GROUPS = ((0, 128),)
 PIECES = ((0, 48), (48, 80))
 H = len(GROUPS)
+CHUNKS = 2
 FAR_FIRST = (8, 7, 9, 6, 10, 5, 11, 4, 12, 3, 13, 2, 14, 1, 15)
 VMEM_BYTES = 63 * 1024 * 1024
 
@@ -48,9 +49,9 @@
 
 
 def kernel(
-    w_ref, emb_ref, len_ref, gw_ref, values_ref, cot_ref, inp_ref, outp_ref,
-    mixed_out, grads_out, proj_out, gwg_out,
-    wbuf, vals, cot, inp, outp, gw, valsp, place, masked, mixed, grads, gradsp, left, acc, gate,
+    w_ref, step_ref, len_ref, gw_ref, values_ref, cot_ref, inp_ref, outp_ref,
+    mixed_out, grads_out, proj_out, left, tbuf_out,
+    wbuf, vals, cot, inp, outp, gw, valsp, place, masked, mixed, grads, gradsp, acc, gate,
     qbuf, psend, precv, eown, erecv, ebuf, tsend, trecv, tbuf,
     l_sem, q_send, q_recv, g_send, g_recv, z_send, z_recv, x_send, x_recv, d_send, d_recv, o_send, o_recv,
     p_send, p_recv, e1_send, e1_recv, e2_send, e2_recv, t1_send, t1_recv, t2_send, t2_recv,
@@ -119,7 +120,9 @@
         copy.start()
         q_copies.append(copy)
 
-    emb = emb_ref[...]
+    counter = lax.broadcasted_iota(jnp.int32, (1, 128), 1).astype(F32)
+    angles = step_ref[0].astype(F32) * jnp.exp(-jnp.log(10000.0) * counter / 128)
+    emb = jnp.concatenate([jnp.cos(angles), jnp.sin(angles)], axis=1)
     loads[0].wait()
     share = jnp.dot(
         jnp.broadcast_to(emb, (8, 256)), gw[...].astype(F32),
@@ -420,42 +423,67 @@
         copy.wait_send()
     for copy in t2_copies:
         copy.wait()
-    grad_all = tbuf[...].reshape(128, 128)
-    for half in range(2):
-        gwg_out[:, 128 * half : 128 * half + 128] = jnp.dot(
-            left[half], grad_all, precision=lax.Precision.HIGHEST, preferred_element_type=F32
-        )
+    tbuf_out[...] = tbuf[...]
     store_mixed.wait()
     store_grads.wait()
 
 
-def frequency_embedding(step_values, freq_width):
-    half_width = freq_width // 2
-    counter = jnp.arange(half_width, dtype=jnp.float32)
-    frequencies = jnp.exp(-jnp.log(10000.0) * counter / half_width)
-    angles = step_values.astype(jnp.float32)[:, None] * frequencies[None, :]
-    return jnp.concatenate([jnp.cos(angles), jnp.sin(angles)], axis=-1)
+def finish(
+    mixed, grads, proj, left, gathered, mixed_out, grads_out, proj_out, gwg_out,
+    mixed_buf, grads_buf, proj_buf, left_buf, gathered_buf, gwg_buf, in_sem, out_sem,
+):
+    small = [
+        pltpu.make_async_copy(left, left_buf, in_sem.at[0]),
+        pltpu.make_async_copy(gathered, gathered_buf, in_sem.at[1]),
+    ]
+    through = [(proj, proj_buf, proj_out)]
+    for n in range(CHUNKS):
+        rows = pl.ds(n * (192 // CHUNKS), 192 // CHUNKS)
+        through.append((mixed.at[rows], mixed_buf.at[rows], mixed_out.at[rows]))
+        through.append((grads.at[rows], grads_buf.at[rows], grads_out.at[rows]))
+    fetches = [
+        pltpu.make_async_copy(a, b, in_sem.at[2 + n]) for n, (a, b, _) in enumerate(through)
+    ]
+    stores = [
+        pltpu.make_async_copy(b, o, out_sem.at[1 + n]) for n, (_, b, o) in enumerate(through)
+    ]
+    for copy in small + fetches:
+        copy.start()
+    for copy in small:
+        copy.wait()
+    grad_all = gathered_buf[...].reshape(128, 128)
+    for half in range(2):
+        gwg_buf[:, 128 * half : 128 * half + 128] = jnp.dot(
+            left_buf[half], grad_all, precision=lax.Precision.HIGHEST, preferred_element_type=F32
+        )
+    gwg_store = pltpu.make_async_copy(gwg_buf, gwg_out, out_sem.at[0])
+    gwg_store.start()
+    for fetch, store in zip(fetches, stores):
+        fetch.wait()
+        store.start()
+    for copy in stores + [gwg_store]:
+        copy.wait()
 
 
 def per_device(
     values, cotangent, out_weight, gate_weight, in_probe, out_probe, timesteps, text_lengths
 ):
-    embedding = frequency_embedding(timesteps, 256)
     vmem = pl.BlockSpec(memory_space=pltpu.VMEM)
     smem = pl.BlockSpec(memory_space=pltpu.SMEM)
     anywhere = pl.BlockSpec(memory_space=pltpu.HBM)
     dma = pltpu.SemaphoreType.DMA
     count = OWN + 1
-    mixed, grads, projected, gwg = pl.pallas_call(
+    mixed, grads, projected, left, gathered = pl.pallas_call(
         kernel,
         out_shape=(
             jax.ShapeDtypeStruct((192, 2048), BF16),
             jax.ShapeDtypeStruct((192, 2048), BF16),
             jax.ShapeDtypeStruct((8, 64), F32),
-            jax.ShapeDtypeStruct((256, 256), F32),
+            jax.ShapeDtypeStruct((2, 256, 128), F32),
+            jax.ShapeDtypeStruct((16, 8, 128), F32),
         ),
-        in_specs=[vmem, vmem, smem, anywhere, anywhere, anywhere, anywhere, anywhere],
-        out_specs=(anywhere, anywhere, vmem, vmem),
+        in_specs=[vmem, smem, smem, anywhere, anywhere, anywhere, anywhere, anywhere],
+        out_specs=(anywhere, anywhere, vmem, vmem, vmem),
         scratch_shapes=[
             pltpu.VMEM((2048, 2048), BF16),
             pltpu.VMEM((192, 2048), BF16),
@@ -469,7 +497,6 @@
             pltpu.VMEM((192, 2048), BF16),
             pltpu.VMEM((192, 2048), BF16),
             pltpu.VMEM((192, 2048), BF16),
-            pltpu.VMEM((2, 256, 128), F32),
             pltpu.VMEM((192, 2048), F32),
             pltpu.VMEM((8, 2048), F32),
             pltpu.VMEM((4, 16, 512), BF16),
@@ -501,9 +528,31 @@
             flops=4 * 192 * 2048 * 2048, bytes_accessed=8 * 192 * 2048, transcendentals=0
         ),
     )(
-        out_weight, embedding, text_lengths, gate_weight,
+        out_weight, timesteps, text_lengths, gate_weight,
         values[0], cotangent[0], in_probe.T, out_probe.T,
     )
+    mixed, grads, projected, gwg = pl.pallas_call(
+        finish,
+        out_shape=(
+            jax.ShapeDtypeStruct((192, 2048), BF16),
+            jax.ShapeDtypeStruct((192, 2048), BF16),
+            jax.ShapeDtypeStruct((8, 64), F32),
+            jax.ShapeDtypeStruct((256, 256), F32),
+        ),
+        in_specs=[anywhere] * 5,
+        out_specs=(anywhere, anywhere, anywhere, anywhere),
+        scratch_shapes=[
+            pltpu.VMEM((192, 2048), BF16),
+            pltpu.VMEM((192, 2048), BF16),
+            pltpu.VMEM((8, 64), F32),
+            pltpu.VMEM((2, 256, 128), F32),
+            pltpu.VMEM((16, 8, 128), F32),
+            pltpu.VMEM((256, 256), F32),
+            dma((3 + 2 * CHUNKS,)),
+            dma((2 + 2 * CHUNKS,)),
+        ],
+        compiler_params=pltpu.CompilerParams(vmem_limit_bytes=VMEM_BYTES),
+    )(mixed, grads, projected, left, gathered)
     return mixed[None], grads[None], projected[None], gwg
 
 

time: 75.2 us -> 72.5 us (0.964)
  local copies, waits for them, and re-layouts: 4.35 us -> 0 us
  Pallas kernels: 68 us -> 70.4 us
    unnamed x10 -> x0, local copies, waits for them, and re-layouts: 4.35 us -> none
    pallas_call x0 -> x1, Pallas kernels: none -> 2.65 us  [per_device(): pl.pallas_call(finish, out_shape=(jax.ShapeDtypeStruct((192, 2048), BF16)...]
where the time goes in v6:
time: 72.5 us; the launch traced here: 72.3 us
  Pallas kernels  70.4 us (97%)
  between operations  1.93 us (3%)
    pallas_call x1, Pallas kernels, per_device(): pl.pallas_call(kernel, out_shape=(jax.ShapeDtypeStruct((192, 2048), BF16)...  67.7 us
    pallas_call x1, Pallas kernels, per_device(): pl.pallas_call(finish, out_shape=(jax.ShapeDtypeStruct((192, 2048), BF16)...  2.65 us

profile of v6, /device:TPU:6, one launch (start us, length us, event | category | flops | bytes accessed | tf_op | source)
XLA Modules:
  0.0 72.3 jit_solution(18444777994631776911)
XLA Ops:
  1.9 67.7 %shard_map.111 = (bf16[192,2048]{1,0:T(8,128)(2,1)}, bf16[192,2048]{1,0:T(8,128)(2,1)}, f32[8,64]{1,0:T(8,128)}, f32[2,256,128]{2,1,0:T(8,128)}, f32[16,8,128]{2,1,0:T(8,128)}) custom-call(bf16[4,2048]{1,0:T(4,128)(2,1)} %w_ref.1, s32[1]{0:T(128)S(6)} %copy.12.step_ref, s32[1]{0:T(128)S(6)} %copy.13.len_ref, bf16[256,256]{1,0:T(8,128)(2,1)} %gw_ref.1, ...), custom_call_target="tpu_custom_call" | custom-call | flops 3221225472 | bytes 3145728 | tf_op jit(solution)/shard_map/pallas_call | solution.py:476
  69.7 2.6 %shard_map.112 = (bf16[192,2048]{1,0:T(8,128)(2,1)}, bf16[192,2048]{1,0:T(8,128)(2,1)}, f32[8,64]{1,0:T(8,128)}, f32[256,256]{1,0:T(8,128)}) custom-call(bf16[192,2048]{1,0:T(8,128)(2,1)} %get-tuple-element.13.mixed, bf16[192,2048]{1,0:T(8,128)(2,1)} %get-tuple-element.14.grads, f32[8,64]{1,0:T(8,128)} %get-tuple-element.15.proj, ...), custom_call_target="tpu_custom_call" | custom-call | tf_op jit(solution)/shard_map/pallas_call | solution.py:534

commit v7 on v6

--- a/solution.py
+++ b/solution.py
@@ -449,6 +449,9 @@
     ]
     for copy in small + fetches:
         copy.start()
+    for fetch, store in zip(fetches, stores):
+        fetch.wait()
+        store.start()
     for copy in small:
         copy.wait()
     grad_all = gathered_buf[...].reshape(128, 128)
@@ -458,9 +461,6 @@
         )
     gwg_store = pltpu.make_async_copy(gwg_buf, gwg_out, out_sem.at[0])
     gwg_store.start()
-    for fetch, store in zip(fetches, stores):
-        fetch.wait()
-        store.start()
     for copy in stores + [gwg_store]:
         copy.wait()
 

time: 72.5 us -> 72.5 us (level)
  no operation moved by 1% of the time
where the time goes in v7:
time: 72.5 us; the launch traced here: 72.3 us
  Pallas kernels  70.4 us (97%)
  between operations  1.93 us (3%)
    pallas_call x1, Pallas kernels, per_device(): pl.pallas_call(kernel, out_shape=(jax.ShapeDtypeStruct((192, 2048), BF16)...  67.7 us
    pallas_call x1, Pallas kernels, per_device(): pl.pallas_call(finish, out_shape=(jax.ShapeDtypeStruct((192, 2048), BF16)...  2.64 us

profile of v7, /device:TPU:6, one launch (start us, length us, event | category | flops | bytes accessed | tf_op | source)
XLA Modules:
  0.0 72.3 jit_solution(7848695140697654011)
XLA Ops:
  1.9 67.7 %shard_map.111 = (bf16[192,2048]{1,0:T(8,128)(2,1)}, bf16[192,2048]{1,0:T(8,128)(2,1)}, f32[8,64]{1,0:T(8,128)}, f32[2,256,128]{2,1,0:T(8,128)}, f32[16,8,128]{2,1,0:T(8,128)}) custom-call(bf16[4,2048]{1,0:T(4,128)(2,1)} %w_ref.1, s32[1]{0:T(128)S(6)} %copy.12.step_ref, s32[1]{0:T(128)S(6)} %copy.13.len_ref, bf16[256,256]{1,0:T(8,128)(2,1)} %gw_ref.1, ...), custom_call_target="tpu_custom_call" | custom-call | flops 3221225472 | bytes 3145728 | tf_op jit(solution)/shard_map/pallas_call | solution.py:476
  69.7 2.6 %shard_map.112 = (bf16[192,2048]{1,0:T(8,128)(2,1)}, bf16[192,2048]{1,0:T(8,128)(2,1)}, f32[8,64]{1,0:T(8,128)}, f32[256,256]{1,0:T(8,128)}) custom-call(bf16[192,2048]{1,0:T(8,128)(2,1)} %get-tuple-element.13.mixed, bf16[192,2048]{1,0:T(8,128)(2,1)} %get-tuple-element.14.grads, f32[8,64]{1,0:T(8,128)} %get-tuple-element.15.proj, ...), custom_call_target="tpu_custom_call" | custom-call | tf_op jit(solution)/shard_map/pallas_call | solution.py:534
